TPU v7x, 256 devices: a whole 4x4x8 slice. The times are simulated.
256 devices in a mesh: occ: 16 (over y, x), aux: 16 (over z, core).
Axes of the slice: x: 4, y: 4, z: 8, core: 2. Of those that a mesh axis runs over, the one named last changes fastest.
Arguments:
- b_factors: bfloat16 [4096, 9216], P('occ', 'aux'), may hold values from -1 to 1, as said below
- occ_energy: float32 [16], P('occ'), may hold values from -1.5 to -0.3
- vir_energy: float32 [256], replicated, may hold values from 0.1 to 2.5
Outputs:
- gamma: float32 [4096, 9216], P('occ', 'aux')
Inputs may be any that keep to these rules, and one draw needn't show every extreme that they name: `b_factors`: real entries; rows are independent of one another.
All inputs are finite; a program needn't handle non-finite values.
Results may differ from a plain program's by a relative error of at most 0.0025.
Values may be sent and summed in bfloat16 or wider, within the bound.
No kernel may reach another device: no remote copies, remote signals or barrier semaphores. Data moves between devices by JAX's collectives and lax.ppermute only.
A program may use at most 64 MiB of HBM per device.

v0:
```python
import functools

import jax
import jax.numpy as jnp
from jax import lax
from jax.experimental import pallas as pl
from jax.experimental.pallas import tpu as pltpu
from jax.sharding import PartitionSpec as P

HELD = (0, 1, 12, 3, 9)
PAIRS = ((0, 0), (0, 1), (0, 2), (1, 2), (1, 3), (0, 3), (3, 4), (0, 4), (1, 4))
ONE_WAY = ((0, 0), (1, 4))
HALF = 16
CHIP = 2 * HALF
SIZE = len(PAIRS) * HALF
VMEM = pl.BlockSpec(memory_space=pltpu.VMEM)
SMEM = pl.BlockSpec(memory_space=pltpu.SMEM)


def send_home(array, by):
    return lax.ppermute(array, "occ", [(i, (i + by) % 16) for i in range(16)])


def along_z(array, hops):
    def target(i):
        return (i // 2 + (hops if i % 2 == 0 else -hops)) % 8 * 2 + i % 2

    return lax.ppermute(array, "aux", [(i, target(i)) for i in range(16)])


def sibling(array):
    return lax.ppermute(array, "aux", [(i, i ^ 1) for i in range(16)])


def place():
    index = lax.axis_index("aux")
    return index // 2, index % 2


def rows_of(chip, half=0):
    return pl.multiple_of((chip + 8) % 8 * CHIP + half * HALF, HALF)


def pack_kernel(b_ref, e_ref, out_ref):
    depth, width = b_ref.shape
    out_ref[:depth] = b_ref[...]
    value = jnp.full((HALF, width), e_ref[0], jnp.float32)
    high = value.astype(jnp.bfloat16)
    rest = value - high.astype(jnp.float32)
    middle = rest.astype(jnp.bfloat16)
    low = (rest - middle.astype(jnp.float32)).astype(jnp.bfloat16)
    row = lax.broadcasted_iota(jnp.int32, value.shape, 0)
    parts = jnp.where(row == 0, high.astype(jnp.float32),
                      jnp.where(row == 1, middle.astype(jnp.float32), low.astype(jnp.float32)))
    out_ref[depth:] = parts.astype(jnp.bfloat16)


def strip_kernel(vir_ref, row_ref, strip_ref, turned):
    row_ref[...] = jnp.broadcast_to(vir_ref[...], row_ref.shape)
    turned[...] = jnp.broadcast_to(vir_ref[...], turned.shape).T
    z, core = place()
    strip_ref[:HALF] = turned[pl.ds(rows_of(z, core), HALF)]
    strip_ref[HALF:] = turned[pl.ds(rows_of(z, 1 - core), HALF)]


def integral_kernel(depth, *refs):
    blocks, keep_ref, send_ref, whole = refs[:5], *refs[5:]
    z, core = place()
    way = 1 - 2 * core
    for r, (first, second) in enumerate(PAIRS):
        whole[...] = lax.dot_general(
            blocks[first][:depth], blocks[second][:depth], (((0,), (0,)), ((), ())),
            preferred_element_type=jnp.float32,
        )
        for k, (hops, side) in enumerate(((1, 0), (1, 1), (2, 0), (2, 1), (3, 0), (3, 1), (4, 0), (0, 0))):
            to = slice(k * SIZE + r * HALF, k * SIZE + (r + 1) * HALF)
            mine, other = (core, 1 - core) if side == 0 else (1 - core, core)
            keep_ref[to] = whole[pl.ds(rows_of(z + way * hops, mine), HALF)]
            send_ref[to] = whole[pl.ds(rows_of(z - way * hops, other), HALF)].astype(jnp.bfloat16)


def core_sum_kernel(keep_ref, got_ref, *out_refs):
    base = 0
    for out in out_refs:
        rows = slice(base, base + out.shape[0])
        out[...] = (keep_ref[rows] + got_ref[rows].astype(jnp.float32)).astype(out.dtype)
        base += out.shape[0]


def relay_kernel(own_ref, three_ref, four_ref, out_ref):
    total = own_ref[...] + three_ref[...].astype(jnp.float32)
    out_ref[:SIZE] = (total[:SIZE] + four_ref[...].astype(jnp.float32)).astype(out_ref.dtype)
    out_ref[SIZE:] = total[SIZE:].astype(out_ref.dtype)


def chip_sum_kernel(own_ref, one_ref, two_ref, out_ref):
    total = one_ref[...].astype(jnp.float32) + two_ref[...].astype(jnp.float32)
    out_ref[:SIZE] = total[:SIZE] + own_ref[...]
    out_ref[SIZE:] = total[SIZE:]


def amplitude_kernel(depth, *refs):
    blocks, mine_ref, other_ref, row_ref, strip_ref, out_ref = refs[:5], *refs[5:]
    levels = []
    for block in blocks:
        parts = block[depth:depth + HALF].astype(jnp.float32)
        levels.append(parts[0:1] + parts[1:2] + parts[2:3])
    for r, (first, second) in enumerate(PAIRS):
        denominator = (strip_ref[...] - levels[first]) + (row_ref[0:1] - levels[second])
        here, there = slice(r * HALF, (r + 1) * HALF), slice(SIZE + r * HALF, SIZE + (r + 1) * HALF)
        out_ref[here] = ((mine_ref[here] + other_ref[there]) / denominator[:HALF]).astype(jnp.bfloat16)
        out_ref[there] = ((mine_ref[there] + other_ref[here]) / denominator[HALF:]).astype(jnp.bfloat16)


def gamma_kernel(depth, *refs):
    blocks, own, mine, other, outs, whole = refs[:5], refs[5], refs[6:10], refs[10:14], refs[14:18], refs[18]
    z, core = place()
    way = 1 - 2 * core
    for r in range(len(PAIRS)):
        for ref, chip, half in (
            [(own, z, core)]
            + [(ref, z - way * hops, core) for hops, ref in enumerate(mine, 1)]
            + [(ref, z + way * hops, 1 - core) for hops, ref in enumerate(other, 1)]
        ):
            whole[r, pl.ds(rows_of(chip, half), HALF)] = ref[r * HALF:(r + 1) * HALF]
            if ref.shape[0] > SIZE:
                whole[r, pl.ds(rows_of(chip, 1 - half), HALF)] = ref[SIZE + r * HALF:SIZE + (r + 1) * HALF]
    gammas(depth, blocks, range(1, 5), whole, outs)


def own_kernel(depth, *refs):
    gammas(depth, refs[:5], (0,), refs[5], refs[6:])


def gammas(depth, blocks, held_blocks, whole, outs):
    for held, out in zip(held_blocks, outs):
        total = None
        for r, (first, second) in enumerate(PAIRS):
            if first == held:
                term = lax.dot_general(
                    blocks[second][:depth], whole[r], (((1,), (1,)), ((), ())), preferred_element_type=jnp.float32
                )
                total = term if total is None else total + term
            if second == held and (first, second) not in ONE_WAY:
                term = lax.dot_general(
                    blocks[first][:depth], whole[r], (((1,), (0,)), ((), ())), preferred_element_type=jnp.float32
                )
                total = term if total is None else total + term
        out[...] = total.astype(out.dtype)


def total_kernel(own_ref, *refs):
    total = own_ref[...]
    for got in refs[:-1]:
        total = total + got[...].astype(jnp.float32)
    refs[-1][...] = total


def call(kernel, ins, out_shape, scratch=()):
    return pl.pallas_call(
        kernel,
        out_shape=out_shape,
        in_specs=ins,
        out_specs=jax.tree.map(lambda _: VMEM, out_shape),
        scratch_shapes=list(scratch),
        compiler_params=pltpu.CompilerParams(vmem_limit_bytes=16 * 1024 * 1024),
    )


def body(b_factors, occ_energy, vir_energy):
    f32, bf16 = jnp.float32, jnp.bfloat16
    shape = jax.ShapeDtypeStruct
    columns = b_factors.T
    depth, width = columns.shape
    square = pltpu.VMEM((width, width), f32)

    packed = call(pack_kernel, [VMEM, SMEM], shape((depth + HALF, width), bf16))(columns, occ_energy)
    blocks = [packed] + [send_home(packed, -s) for s in HELD[1:]]

    row, strip = call(strip_kernel, [VMEM], [shape((8, width), f32), shape((CHIP, width), f32)], [square])(
        vir_energy[None, :]
    )

    keep, send = call(
        functools.partial(integral_kernel, depth), [VMEM] * 5,
        [shape((8 * SIZE, width), f32), shape((8 * SIZE, width), bf16)], [square],
    )(*blocks)
    one, two, three, four, own = call(
        core_sum_kernel, [VMEM] * 2,
        [shape((n * SIZE, width), t) for n, t in ((2, bf16), (2, f32), (2, bf16), (1, bf16), (1, f32))],
    )(keep, sibling(send))
    four = along_z(four, 2)
    three = along_z(three, 1)
    one = along_z(one, 1)
    two = along_z(call(relay_kernel, [VMEM] * 3, shape((2 * SIZE, width), bf16))(two, three, four), 2)
    partial = call(chip_sum_kernel, [VMEM] * 3, shape((2 * SIZE, width), f32))(own, one, two)

    amplitude = call(functools.partial(amplitude_kernel, depth), [VMEM] * 9, shape((2 * SIZE, width), bf16))(
        *blocks, partial, sibling(partial), row, strip
    )
    two = along_z(amplitude, 2)
    one = along_z(amplitude, 1)
    three = along_z(two, 1)
    four = along_z(two[:SIZE], 2)
    mine = [one, two, three, four]
    other = [sibling(piece) for piece in mine]

    parts = call(
        functools.partial(gamma_kernel, depth),
        [VMEM] * 14,
        [shape((depth, width), bf16)] * 4 + [shape((len(PAIRS), width, width), bf16)],
    )(*blocks, amplitude, *mine, *other)
    *parts, whole = parts
    own = call(functools.partial(own_kernel, depth), [VMEM] * 6, [shape((depth, width), f32)])(*blocks, whole)[0]

    back = [send_home(parts[k - 1], HELD[k]) for k in (4, 3, 2, 1)]
    return call(total_kernel, [VMEM] * 5, shape((depth, width), f32))(own, *back).T


def solution(mesh):
    placed = (P("occ", "aux"), P("occ"), P())
    return jax.shard_map(
        body, mesh=mesh, in_specs=placed, out_specs=P("occ", "aux"), check_vma=False
    )
```

profile of v0, /device:TPU:1, one launch (start us, length us, event | category | flops | bytes accessed | tf_op | source)
XLA Modules:
  0.0 86.9 jit_solution(10602114813432997290)
XLA Ops:
  1.6 4.4 %collective-permute-start.3 = (bf16[592,256]{1,0:T(8,128)(2,1)S(1)}, bf16[592,256]{1,0:T(8,128)(2,1)S(1)}, u32[]{:S(2)}, u32[]{:S(2)}) collective-permute-start(bf16[592,256]{1,0:T(8,128)(2,1)S(1)} %shard_map.37.refs_0_), channel_id=1, source_target_pairs={{0,112},{16,128},{32,144},{48,160},{64,176},{80,192},{96,208},{112... | collective-permute-start | bytes 909320 | tf_op jit(solution)/shard_map/ppermute | solution.py:21
  7.8 3.3 %collective-permute-start = (bf16[592,256]{1,0:T(8,128)(2,1)S(1)}, bf16[592,256]{1,0:T(8,128)(2,1)S(1)}, u32[]{:S(2)}, u32[]{:S(2)}) collective-permute-start(bf16[592,256]{1,0:T(8,128)(2,1)S(1)} %shard_map.37.refs_0_), channel_id=1, source_target_pairs={{0,240},{16,0},{32,16},{48,32},{64,48},{80,64},{96,80},{112,96},{1... | collective-permute-start | bytes 909320 | tf_op jit(solution)/shard_map/ppermute | solution.py:21
  11.9 5.1 %collective-permute-done.2.refs_3_ = bf16[592,256]{1,0:T(8,128)(2,1)S(1)} collective-permute-done((bf16[592,256]{1,0:T(8,128)(2,1)S(1)}, bf16[592,256]{1,0:T(8,128)(2,1)S(1)}, u32[]{:S(2)}, u32[]{:S(2)}) %collective-permute-start.2) | collective-permute-done | bytes 303136 | tf_op jit(solution)/shard_map/ppermute | solution.py:21
  17.0 3.0 %collective-permute-done.1.refs_2_ = bf16[592,256]{1,0:T(8,128)(2,1)S(1)} collective-permute-done((bf16[592,256]{1,0:T(8,128)(2,1)S(1)}, bf16[592,256]{1,0:T(8,128)(2,1)S(1)}, u32[]{:S(2)}, u32[]{:S(2)}) %collective-permute-start.1) | collective-permute-done | bytes 303136 | tf_op jit(solution)/shard_map/ppermute | solution.py:21
  20.0 1.3 %shard_map.38 = (f32[1152,256]{1,0:T(8,128)S(1)}, bf16[1152,256]{1,0:T(8,128)(2,1)S(1)}) custom-call(bf16[592,256]{1,0:T(8,128)(2,1)S(1)} %shard_map.37.refs_0_, bf16[592,256]{1,0:T(8,128)(2,1)S(1)} %collective-permute-done.refs_1_, bf16[592,256]{1,0:T(8,128)(2,1)S(1)} %collective-permute-done.1.refs_2_, ...), custom_call_target="tpu_custom_call" | custom-call | tf_op jit(solution)/shard_map/pallas_call | solution.py:184
  21.3 1.4 %collective-permute-start.4 = (bf16[1152,256]{1,0:T(8,128)(2,1)S(1)}, bf16[1152,256]{1,0:T(8,128)(2,1)S(1)}, u32[]{:S(2)}, u32[]{:S(2)}) collective-permute-start(bf16[1152,256]{1,0:T(8,128)(2,1)S(1)} %get-tuple-element.20), channel_id=1, source_target_pairs={{0,1},{1,0},{2,3},{3,2},{4,5},{5,4},{6,7},{7,6},{8,9},{9,8},{10,11... | collective-permute-start | bytes 1769480 | tf_op jit(solution)/shard_map/ppermute | solution.py:32
  22.7 1.6 %collective-permute-done.4.got_ref = bf16[1152,256]{1,0:T(8,128)(2,1)S(1)} collective-permute-done((bf16[1152,256]{1,0:T(8,128)(2,1)S(1)}, bf16[1152,256]{1,0:T(8,128)(2,1)S(1)}, u32[]{:S(2)}, u32[]{:S(2)}) %collective-permute-start.4) | collective-permute-done | bytes 589856 | tf_op jit(solution)/shard_map/ppermute | solution.py:32
  24.5 5.6 %collective-permute-start.6 = (bf16[288,256]{1,0:T(8,128)(2,1)S(1)}, bf16[288,256]{1,0:T(8,128)(2,1)S(1)}, u32[]{:S(2)}, u32[]{:S(2)}) collective-permute-start(bf16[288,256]{1,0:T(8,128)(2,1)S(1)} %get-tuple-element.24), channel_id=1, source_target_pairs={{0,2},{1,15},{2,4},{3,1},{4,6},{5,3},{6,8},{7,5},{8,10},{9,7},{10,... | collective-permute-start | bytes 442376 | tf_op jit(solution)/shard_map/ppermute | solution.py:28
  32.0 2.5 %collective-permute-done.7.four_ref = bf16[144,256]{1,0:T(8,128)(2,1)S(1)} collective-permute-done((bf16[144,256]{1,0:T(8,128)(2,1)S(1)}, bf16[144,256]{1,0:T(8,128)(2,1)S(1)}, u32[]{:S(2)}, u32[]{:S(2)}) %collective-permute-start.7) | collective-permute-done | bytes 73760 | tf_op jit(solution)/shard_map/ppermute | solution.py:28
  34.5 3.2 %collective-permute-start.8 = (bf16[288,256]{1,0:T(8,128)(2,1)S(1)}, bf16[288,256]{1,0:T(8,128)(2,1)S(1)}, u32[]{:S(2)}, u32[]{:S(2)}) collective-permute-start(bf16[288,256]{1,0:T(8,128)(2,1)S(1)} %shard_map.40), channel_id=1, source_target_pairs={{0,4},{1,13},{2,6},{3,15},{4,8},{5,1},{6,10},{7,3},{8,12},{9,5},{1... | collective-permute-start | bytes 442376 | tf_op jit(solution)/shard_map/ppermute | solution.py:28
  37.8 3.4 %collective-permute-done.8.two_ref = bf16[288,256]{1,0:T(8,128)(2,1)S(1)} collective-permute-done((bf16[288,256]{1,0:T(8,128)(2,1)S(1)}, bf16[288,256]{1,0:T(8,128)(2,1)S(1)}, u32[]{:S(2)}, u32[]{:S(2)}) %collective-permute-start.8) | collective-permute-done | bytes 147488 | tf_op jit(solution)/shard_map/ppermute | solution.py:28
  41.2 4.6 %collective-permute-start.9 = (f32[288,256]{1,0:T(8,128)S(1)}, f32[288,256]{1,0:T(8,128)S(1)}, u32[]{:S(2)}, u32[]{:S(2)}) collective-permute-start(f32[288,256]{1,0:T(8,128)S(1)} %shard_map.41.refs_5_), channel_id=1, source_target_pairs={{0,1},{1,0},{2,3},{3,2},{4,5},{5,4},{6,7},{7,6},{8,9},{9,8},{10,11... | collective-permute-start | bytes 884744 | tf_op jit(solution)/shard_map/ppermute | solution.py:32
  47.1 1.7 %collective-permute-start.10 = (bf16[288,256]{1,0:T(8,128)(2,1)S(1)}, bf16[288,256]{1,0:T(8,128)(2,1)S(1)}, u32[]{:S(2)}, u32[]{:S(2)}) collective-permute-start(bf16[288,256]{1,0:T(8,128)(2,1)S(1)} %shard_map.43.refs_5_), channel_id=1, source_target_pairs={{0,2},{1,15},{2,4},{3,1},{4,6},{5,3},{6,8},{7,5},{8,10},{9,7},{10,... | collective-permute-start | bytes 442376 | tf_op jit(solution)/shard_map/ppermute | solution.py:28
  48.8 3.5 %collective-permute-done.11.refs_7_ = bf16[288,256]{1,0:T(8,128)(2,1)S(1)} collective-permute-done((bf16[288,256]{1,0:T(8,128)(2,1)S(1)}, bf16[288,256]{1,0:T(8,128)(2,1)S(1)}, u32[]{:S(2)}, u32[]{:S(2)}) %collective-permute-start.11) | collective-permute-done | bytes 147488 | tf_op jit(solution)/shard_map/ppermute | solution.py:28
  52.3 2.6 %collective-permute-start.12 = (bf16[288,256]{1,0:T(8,128)(2,1)S(1)}, bf16[288,256]{1,0:T(8,128)(2,1)S(1)}, u32[]{:S(2)}, u32[]{:S(2)}) collective-permute-start(bf16[288,256]{1,0:T(8,128)(2,1)S(1)} %collective-permute-done.11.refs_7_), channel_id=1, source_target_pairs={{0,2},{1,15},{2,4},{3,1},{4,6},{5,3},{6,8},{7,5},{8,10},{9,7},{10,... | collective-permute-start | bytes 442376 | tf_op jit(solution)/shard_map/ppermute | solution.py:28
  56.0 1.8 %collective-permute-done.12.refs_8_ = bf16[288,256]{1,0:T(8,128)(2,1)S(1)} collective-permute-done((bf16[288,256]{1,0:T(8,128)(2,1)S(1)}, bf16[288,256]{1,0:T(8,128)(2,1)S(1)}, u32[]{:S(2)}, u32[]{:S(2)}) %collective-permute-start.12) | collective-permute-done | bytes 147488 | tf_op jit(solution)/shard_map/ppermute | solution.py:28
  57.8 4.8 %collective-permute-start.16 = (bf16[288,256]{1,0:T(8,128)(2,1)S(1)}, bf16[288,256]{1,0:T(8,128)(2,1)S(1)}, u32[]{:S(2)}, u32[]{:S(2)}) collective-permute-start(bf16[288,256]{1,0:T(8,128)(2,1)S(1)} %collective-permute-done.12.refs_8_), channel_id=1, source_target_pairs={{0,1},{1,0},{2,3},{3,2},{4,5},{5,4},{6,7},{7,6},{8,9},{9,8},{10,11... | collective-permute-start | bytes 442376 | tf_op jit(solution)/shard_map/ppermute | solution.py:32
  62.6 1.3 %collective-permute-done.17.refs_13_ = bf16[144,256]{1,0:T(8,128)(2,1)S(1)} collective-permute-done((bf16[144,256]{1,0:T(8,128)(2,1)S(1)}, bf16[144,256]{1,0:T(8,128)(2,1)S(1)}, u32[]{:S(2)}, u32[]{:S(2)}) %collective-permute-start.17) | collective-permute-done | bytes 73760 | tf_op jit(solution)/shard_map/ppermute | solution.py:32
  65.1 3.6 %collective-permute-start.18 = (bf16[576,256]{1,0:T(8,128)(2,1)S(1)}, bf16[576,256]{1,0:T(8,128)(2,1)S(1)}, u32[]{:S(2)}, u32[]{:S(2)}) collective-permute-start(bf16[576,256]{1,0:T(8,128)(2,1)S(1)} %get-tuple-element.29), channel_id=1, source_target_pairs={{0,144},{16,160},{32,176},{48,192},{64,208},{80,224},{96,240},{112... | collective-permute-start | bytes 884744 | tf_op jit(solution)/shard_map/ppermute | solution.py:21
  69.1 3.0 %collective-permute-start.20 = (bf16[576,256]{1,0:T(8,128)(2,1)S(1)}, bf16[576,256]{1,0:T(8,128)(2,1)S(1)}, u32[]{:S(2)}, u32[]{:S(2)}) collective-permute-start(bf16[576,256]{1,0:T(8,128)(2,1)S(1)} %get-tuple-element.31), channel_id=1, source_target_pairs={{0,192},{16,208},{32,224},{48,240},{64,0},{80,16},{96,32},{112,48}... | collective-permute-start | bytes 884744 | tf_op jit(solution)/shard_map/ppermute | solution.py:21
  73.9 3.6 %collective-permute-done.18.refs_0_ = bf16[576,256]{1,0:T(8,128)(2,1)S(1)} collective-permute-done((bf16[576,256]{1,0:T(8,128)(2,1)S(1)}, bf16[576,256]{1,0:T(8,128)(2,1)S(1)}, u32[]{:S(2)}, u32[]{:S(2)}) %collective-permute-start.18) | collective-permute-done | bytes 294944 | tf_op jit(solution)/shard_map/ppermute | solution.py:21
  77.5 4.3 %collective-permute-done.19.refs_1_ = bf16[576,256]{1,0:T(8,128)(2,1)S(1)} collective-permute-done((bf16[576,256]{1,0:T(8,128)(2,1)S(1)}, bf16[576,256]{1,0:T(8,128)(2,1)S(1)}, u32[]{:S(2)}, u32[]{:S(2)}) %collective-permute-start.19) | collective-permute-done | bytes 294944 | tf_op jit(solution)/shard_map/ppermute | solution.py:21
  81.8 1.3 %collective-permute-done.20.refs_2_ = bf16[576,256]{1,0:T(8,128)(2,1)S(1)} collective-permute-done((bf16[576,256]{1,0:T(8,128)(2,1)S(1)}, bf16[576,256]{1,0:T(8,128)(2,1)S(1)}, u32[]{:S(2)}, u32[]{:S(2)}) %collective-permute-start.20) | collective-permute-done | bytes 294944 | tf_op jit(solution)/shard_map/ppermute | solution.py:21
  83.1 2.8 %collective-permute-done.21.refs_3_ = bf16[576,256]{1,0:T(8,128)(2,1)S(1)} collective-permute-done((bf16[576,256]{1,0:T(8,128)(2,1)S(1)}, bf16[576,256]{1,0:T(8,128)(2,1)S(1)}, u32[]{:S(2)}, u32[]{:S(2)}) %collective-permute-start.21) | collective-permute-done | bytes 294944 | tf_op jit(solution)/shard_map/ppermute | solution.py:21
  (35 shorter events, 12.4 us)
Async XLA Ops:
  0.7 1.0 %copy-start = (bf16[256,576]{0,1:T(8,128)(2,1)S(1)}, bf16[256,576]{0,1:T(8,128)(2,1)}, u32[]{:S(2)}) copy-start(bf16[256,576]{0,1:T(8,128)(2,1)} %param.3) | copy-start | bytes 884740
  1.6 10.3 %collective-permute-start.3 = (bf16[592,256]{1,0:T(8,128)(2,1)S(1)}, bf16[592,256]{1,0:T(8,128)(2,1)S(1)}, u32[]{:S(2)}, u32[]{:S(2)}) collective-permute-start(bf16[592,256]{1,0:T(8,128)(2,1)S(1)} %shard_map.37.refs_0_), channel_id=1, source_target_pairs={{0,112},{16,128},{32,144},{48,160},{64,176},{80,192},{96,208},{112... | collective-permute-start | bytes 909320 | tf_op jit(solution)/shard_map/ppermute | solution.py:21
  6.0 11.0 %collective-permute-start.2 = (bf16[592,256]{1,0:T(8,128)(2,1)S(1)}, bf16[592,256]{1,0:T(8,128)(2,1)S(1)}, u32[]{:S(2)}, u32[]{:S(2)}) collective-permute-start(bf16[592,256]{1,0:T(8,128)(2,1)S(1)} %shard_map.37.refs_0_), channel_id=1, source_target_pairs={{0,208},{16,224},{32,240},{48,0},{64,16},{80,32},{96,48},{112,64},... | collective-permute-start | bytes 909320 | tf_op jit(solution)/shard_map/ppermute | solution.py:21
  7.1 12.8 %collective-permute-start.1 = (bf16[592,256]{1,0:T(8,128)(2,1)S(1)}, bf16[592,256]{1,0:T(8,128)(2,1)S(1)}, u32[]{:S(2)}, u32[]{:S(2)}) collective-permute-start(bf16[592,256]{1,0:T(8,128)(2,1)S(1)} %shard_map.37.refs_0_), channel_id=1, source_target_pairs={{0,64},{16,80},{32,96},{48,112},{64,128},{80,144},{96,160},{112,17... | collective-permute-start | bytes 909320 | tf_op jit(solution)/shard_map/ppermute | solution.py:21
  7.8 12.1 %collective-permute-start = (bf16[592,256]{1,0:T(8,128)(2,1)S(1)}, bf16[592,256]{1,0:T(8,128)(2,1)S(1)}, u32[]{:S(2)}, u32[]{:S(2)}) collective-permute-start(bf16[592,256]{1,0:T(8,128)(2,1)S(1)} %shard_map.37.refs_0_), channel_id=1, source_target_pairs={{0,240},{16,0},{32,16},{48,32},{64,48},{80,64},{96,80},{112,96},{1... | collective-permute-start | bytes 909320 | tf_op jit(solution)/shard_map/ppermute | solution.py:21
  21.3 3.1 %collective-permute-start.4 = (bf16[1152,256]{1,0:T(8,128)(2,1)S(1)}, bf16[1152,256]{1,0:T(8,128)(2,1)S(1)}, u32[]{:S(2)}, u32[]{:S(2)}) collective-permute-start(bf16[1152,256]{1,0:T(8,128)(2,1)S(1)} %get-tuple-element.20), channel_id=1, source_target_pairs={{0,1},{1,0},{2,3},{3,2},{4,5},{5,4},{6,7},{7,6},{8,9},{9,8},{10,11... | collective-permute-start | bytes 1769480 | tf_op jit(solution)/shard_map/ppermute | solution.py:32
  24.3 21.4 %copy-start.1 = (f32[256]{0:T(256)S(1)}, f32[256]{0:T(256)}, u32[]{:S(2)}) copy-start(f32[256]{0:T(256)} %param.5) | copy-start | bytes 3076
  24.5 10.1 %collective-permute-start.6 = (bf16[288,256]{1,0:T(8,128)(2,1)S(1)}, bf16[288,256]{1,0:T(8,128)(2,1)S(1)}, u32[]{:S(2)}, u32[]{:S(2)}) collective-permute-start(bf16[288,256]{1,0:T(8,128)(2,1)S(1)} %get-tuple-element.24), channel_id=1, source_target_pairs={{0,2},{1,15},{2,4},{3,1},{4,6},{5,3},{6,8},{7,5},{8,10},{9,7},{10,... | collective-permute-start | bytes 442376 | tf_op jit(solution)/shard_map/ppermute | solution.py:28
  30.1 4.4 %collective-permute-start.7 = (bf16[144,256]{1,0:T(8,128)(2,1)S(1)}, bf16[144,256]{1,0:T(8,128)(2,1)S(1)}, u32[]{:S(2)}, u32[]{:S(2)}) collective-permute-start(bf16[144,256]{1,0:T(8,128)(2,1)S(1)} %get-tuple-element.25), channel_id=1, source_target_pairs={{0,4},{1,13},{2,6},{3,15},{4,8},{5,1},{6,10},{7,3},{8,12},{9,5},{1... | collective-permute-start | bytes 221192 | tf_op jit(solution)/shard_map/ppermute | solution.py:28
  31.3 6.5 %collective-permute-start.5 = (bf16[288,256]{1,0:T(8,128)(2,1)S(1)}, bf16[288,256]{1,0:T(8,128)(2,1)S(1)}, u32[]{:S(2)}, u32[]{:S(2)}) collective-permute-start(bf16[288,256]{1,0:T(8,128)(2,1)S(1)} %get-tuple-element.22), channel_id=1, source_target_pairs={{0,2},{1,15},{2,4},{3,1},{4,6},{5,3},{6,8},{7,5},{8,10},{9,7},{10,... | collective-permute-start | bytes 442376 | tf_op jit(solution)/shard_map/ppermute | solution.py:28
  34.5 6.6 %collective-permute-start.8 = (bf16[288,256]{1,0:T(8,128)(2,1)S(1)}, bf16[288,256]{1,0:T(8,128)(2,1)S(1)}, u32[]{:S(2)}, u32[]{:S(2)}) collective-permute-start(bf16[288,256]{1,0:T(8,128)(2,1)S(1)} %shard_map.40), channel_id=1, source_target_pairs={{0,4},{1,13},{2,6},{3,15},{4,8},{5,1},{6,10},{7,3},{8,12},{9,5},{1... | collective-permute-start | bytes 442376 | tf_op jit(solution)/shard_map/ppermute | solution.py:28
  41.2 5.8 %collective-permute-start.9 = (f32[288,256]{1,0:T(8,128)S(1)}, f32[288,256]{1,0:T(8,128)S(1)}, u32[]{:S(2)}, u32[]{:S(2)}) collective-permute-start(f32[288,256]{1,0:T(8,128)S(1)} %shard_map.41.refs_5_), channel_id=1, source_target_pairs={{0,1},{1,0},{2,3},{3,2},{4,5},{5,4},{6,7},{7,6},{8,9},{9,8},{10,11... | collective-permute-start | bytes 884744 | tf_op jit(solution)/shard_map/ppermute | solution.py:32
  47.0 5.3 %collective-permute-start.11 = (bf16[288,256]{1,0:T(8,128)(2,1)S(1)}, bf16[288,256]{1,0:T(8,128)(2,1)S(1)}, u32[]{:S(2)}, u32[]{:S(2)}) collective-permute-start(bf16[288,256]{1,0:T(8,128)(2,1)S(1)} %shard_map.43.refs_5_), channel_id=1, source_target_pairs={{0,4},{1,13},{2,6},{3,15},{4,8},{5,1},{6,10},{7,3},{8,12},{9,5},{1... | collective-permute-start | bytes 442376 | tf_op jit(solution)/shard_map/ppermute | solution.py:28
  47.1 8.7 %collective-permute-start.10 = (bf16[288,256]{1,0:T(8,128)(2,1)S(1)}, bf16[288,256]{1,0:T(8,128)(2,1)S(1)}, u32[]{:S(2)}, u32[]{:S(2)}) collective-permute-start(bf16[288,256]{1,0:T(8,128)(2,1)S(1)} %shard_map.43.refs_5_), channel_id=1, source_target_pairs={{0,2},{1,15},{2,4},{3,1},{4,6},{5,3},{6,8},{7,5},{8,10},{9,7},{10,... | collective-permute-start | bytes 442376 | tf_op jit(solution)/shard_map/ppermute | solution.py:28
  52.3 5.5 %collective-permute-start.12 = (bf16[288,256]{1,0:T(8,128)(2,1)S(1)}, bf16[288,256]{1,0:T(8,128)(2,1)S(1)}, u32[]{:S(2)}, u32[]{:S(2)}) collective-permute-start(bf16[288,256]{1,0:T(8,128)(2,1)S(1)} %collective-permute-done.11.refs_7_), channel_id=1, source_target_pairs={{0,2},{1,15},{2,4},{3,1},{4,6},{5,3},{6,8},{7,5},{8,10},{9,7},{10,... | collective-permute-start | bytes 442376 | tf_op jit(solution)/shard_map/ppermute | solution.py:28
  54.9 7.7 %collective-permute-start.13 = (bf16[144,256]{1,0:T(8,128)(2,1)S(1)}, bf16[144,256]{1,0:T(8,128)(2,1)S(1)}, u32[]{:S(2)}, u32[]{:S(2)}) collective-permute-start(bf16[144,256]{1,0:T(8,128)(2,1)S(1)} %slice.4), channel_id=1, source_target_pairs={{0,4},{1,13},{2,6},{3,15},{4,8},{5,1},{6,10},{7,3},{8,12},{9,5},{1... | collective-permute-start | bytes 221192 | tf_op jit(solution)/shard_map/ppermute | solution.py:28
  55.0 8.9 %collective-permute-start.15 = (bf16[288,256]{1,0:T(8,128)(2,1)S(1)}, bf16[288,256]{1,0:T(8,128)(2,1)S(1)}, u32[]{:S(2)}, u32[]{:S(2)}) collective-permute-start(bf16[288,256]{1,0:T(8,128)(2,1)S(1)} %collective-permute-done.11.refs_7_), channel_id=1, source_target_pairs={{0,1},{1,0},{2,3},{3,2},{4,5},{5,4},{6,7},{7,6},{8,9},{9,8},{10,11... | collective-permute-start | bytes 442376 | tf_op jit(solution)/shard_map/ppermute | solution.py:32
  55.8 8.0 %collective-permute-start.14 = (bf16[288,256]{1,0:T(8,128)(2,1)S(1)}, bf16[288,256]{1,0:T(8,128)(2,1)S(1)}, u32[]{:S(2)}, u32[]{:S(2)}) collective-permute-start(bf16[288,256]{1,0:T(8,128)(2,1)S(1)} %collective-permute-done.10.refs_6_), channel_id=1, source_target_pairs={{0,1},{1,0},{2,3},{3,2},{4,5},{5,4},{6,7},{7,6},{8,9},{9,8},{10,11... | collective-permute-start | bytes 442376 | tf_op jit(solution)/shard_map/ppermute | solution.py:32
  57.8 6.1 %collective-permute-start.16 = (bf16[288,256]{1,0:T(8,128)(2,1)S(1)}, bf16[288,256]{1,0:T(8,128)(2,1)S(1)}, u32[]{:S(2)}, u32[]{:S(2)}) collective-permute-start(bf16[288,256]{1,0:T(8,128)(2,1)S(1)} %collective-permute-done.12.refs_8_), channel_id=1, source_target_pairs={{0,1},{1,0},{2,3},{3,2},{4,5},{5,4},{6,7},{7,6},{8,9},{9,8},{10,11... | collective-permute-start | bytes 442376 | tf_op jit(solution)/shard_map/ppermute | solution.py:32
  62.6 1.3 %collective-permute-start.17 = (bf16[144,256]{1,0:T(8,128)(2,1)S(1)}, bf16[144,256]{1,0:T(8,128)(2,1)S(1)}, u32[]{:S(2)}, u32[]{:S(2)}) collective-permute-start(bf16[144,256]{1,0:T(8,128)(2,1)S(1)} %collective-permute-done.13.refs_9_), channel_id=1, source_target_pairs={{0,1},{1,0},{2,3},{3,2},{4,5},{5,4},{6,7},{7,6},{8,9},{9,8},{10,11... | collective-permute-start | bytes 221192 | tf_op jit(solution)/shard_map/ppermute | solution.py:32
  65.1 12.4 %collective-permute-start.18 = (bf16[576,256]{1,0:T(8,128)(2,1)S(1)}, bf16[576,256]{1,0:T(8,128)(2,1)S(1)}, u32[]{:S(2)}, u32[]{:S(2)}) collective-permute-start(bf16[576,256]{1,0:T(8,128)(2,1)S(1)} %get-tuple-element.29), channel_id=1, source_target_pairs={{0,144},{16,160},{32,176},{48,192},{64,208},{80,224},{96,240},{112... | collective-permute-start | bytes 884744 | tf_op jit(solution)/shard_map/ppermute | solution.py:21
  68.7 13.1 %collective-permute-start.19 = (bf16[576,256]{1,0:T(8,128)(2,1)S(1)}, bf16[576,256]{1,0:T(8,128)(2,1)S(1)}, u32[]{:S(2)}, u32[]{:S(2)}) collective-permute-start(bf16[576,256]{1,0:T(8,128)(2,1)S(1)} %get-tuple-element.30), channel_id=1, source_target_pairs={{0,48},{16,64},{32,80},{48,96},{64,112},{80,128},{96,144},{112,160... | collective-permute-start | bytes 884744 | tf_op jit(solution)/shard_map/ppermute | solution.py:21
  69.1 14.0 %collective-permute-start.20 = (bf16[576,256]{1,0:T(8,128)(2,1)S(1)}, bf16[576,256]{1,0:T(8,128)(2,1)S(1)}, u32[]{:S(2)}, u32[]{:S(2)}) collective-permute-start(bf16[576,256]{1,0:T(8,128)(2,1)S(1)} %get-tuple-element.31), channel_id=1, source_target_pairs={{0,192},{16,208},{32,224},{48,240},{64,0},{80,16},{96,32},{112,48}... | collective-permute-start | bytes 884744 | tf_op jit(solution)/shard_map/ppermute | solution.py:21
  72.1 13.8 %collective-permute-start.21 = (bf16[576,256]{1,0:T(8,128)(2,1)S(1)}, bf16[576,256]{1,0:T(8,128)(2,1)S(1)}, u32[]{:S(2)}, u32[]{:S(2)}) collective-permute-start(bf16[576,256]{1,0:T(8,128)(2,1)S(1)} %get-tuple-element.32), channel_id=1, source_target_pairs={{0,16},{16,32},{32,48},{48,64},{64,80},{80,96},{96,112},{112,128},... | collective-permute-start | bytes 884744 | tf_op jit(solution)/shard_map/ppermute | solution.py:21
where the time goes:
time: 87 us; the launch traced here: 86.9 us
  starting transfers between devices  44.7 us (51%)
  waiting for transfers between devices  36.1 us (41%)
  Pallas kernels  4.39 us (5%)
  local copies, waits for them, and re-layouts  0.96 us (1%)
    ppermute x8, waiting for transfers between devices, send_home(): return lax.ppermute(array, 'occ', [(i, (i + by) % 16) for i in range(16)])  20.8 us
    ppermute x8, starting transfers between devices, send_home(): return lax.ppermute(array, 'occ', [(i, (i + by) % 16) for i in range(16)])  17.7 us
    ppermute x8, starting transfers between devices, along_z(): return lax.ppermute(array, 'aux', [(i, target(i)) for i in range(16)])  15.2 us
    ppermute x6, starting transfers between devices, sibling(): return lax.ppermute(array, 'aux', [(i, i ^ 1) for i in range(16)])  11.8 us
    ppermute x8, waiting for transfers between devices, along_z(): return lax.ppermute(array, 'aux', [(i, target(i)) for i in range(16)])  11.3 us
    ppermute x6, waiting for transfers between devices, sibling(): return lax.ppermute(array, 'aux', [(i, i ^ 1) for i in range(16)])  4 us
  transfers between devices with their start and end apart: 22, of which 14 were waited for; matrix products, arithmetic and copies ran while one was open for 0% of the time, Pallas kernels for 1%

commit v1 on v0

--- a/solution.py
+++ b/solution.py
@@ -8,7 +8,8 @@
 from jax.sharding import PartitionSpec as P
 
 HELD = (0, 1, 12, 3, 9)
-PAIRS = ((0, 0), (0, 1), (0, 2), (1, 2), (1, 3), (0, 3), (3, 4), (0, 4), (1, 4))
+PAIRS = ((0, 0), (0, 3), (3, 4), (0, 4), (0, 1), (0, 2), (1, 2), (1, 3), (1, 4))
+EARLY = 4
 ONE_WAY = ((0, 0), (1, 4))
 HALF = 16
 CHIP = 2 * HALF
@@ -63,20 +64,31 @@
     strip_ref[HALF:] = turned[pl.ds(rows_of(z, 1 - core), HALF)]
 
 
-def integral_kernel(depth, *refs):
-    blocks, keep_ref, send_ref, whole = refs[:5], *refs[5:]
+def integrals(depth, blocks, pairs, keep_ref, send_ref, whole, size):
     z, core = place()
     way = 1 - 2 * core
-    for r, (first, second) in enumerate(PAIRS):
-        whole[...] = lax.dot_general(
-            blocks[first][:depth], blocks[second][:depth], (((0,), (0,)), ((), ())),
-            preferred_element_type=jnp.float32,
-        )
+    turned = {first: blocks[first][:depth].T for first in {PAIRS[r][0]: None for r in pairs}}
+    for r in pairs:
+        first, second = PAIRS[r]
+        whole[...] = jnp.dot(turned[first], blocks[second][:depth], preferred_element_type=jnp.float32)
         for k, (hops, side) in enumerate(((1, 0), (1, 1), (2, 0), (2, 1), (3, 0), (3, 1), (4, 0), (0, 0))):
-            to = slice(k * SIZE + r * HALF, k * SIZE + (r + 1) * HALF)
+            to = slice(k * size + r * HALF, k * size + (r + 1) * HALF)
             mine, other = (core, 1 - core) if side == 0 else (1 - core, core)
             keep_ref[to] = whole[pl.ds(rows_of(z + way * hops, mine), HALF)]
             send_ref[to] = whole[pl.ds(rows_of(z - way * hops, other), HALF)].astype(jnp.bfloat16)
+
+
+def early_kernel(depth, own_ref, third_ref, fourth_ref, keep_ref, send_ref, whole):
+    integrals(depth, {0: own_ref, 3: third_ref, 4: fourth_ref}, range(EARLY), keep_ref, send_ref, whole, EARLY * HALF)
+
+
+def late_kernel(depth, *refs):
+    early_keep, early_send, keep_ref, send_ref, whole = refs[5:]
+    size = EARLY * HALF
+    for k in range(8):
+        keep_ref[k * SIZE:k * SIZE + size] = early_keep[k * size:(k + 1) * size]
+        send_ref[k * SIZE:k * SIZE + size] = early_send[k * size:(k + 1) * size]
+    integrals(depth, refs[:5], range(EARLY, len(PAIRS)), keep_ref, send_ref, whole, SIZE)
 
 
 def core_sum_kernel(keep_ref, got_ref, *out_refs):
@@ -149,13 +161,6 @@
         out[...] = total.astype(out.dtype)
 
 
-def total_kernel(own_ref, *refs):
-    total = own_ref[...]
-    for got in refs[:-1]:
-        total = total + got[...].astype(jnp.float32)
-    refs[-1][...] = total
-
-
 def call(kernel, ins, out_shape, scratch=()):
     return pl.pallas_call(
         kernel,
@@ -181,10 +186,13 @@
         vir_energy[None, :]
     )
 
-    keep, send = call(
-        functools.partial(integral_kernel, depth), [VMEM] * 5,
-        [shape((8 * SIZE, width), f32), shape((8 * SIZE, width), bf16)], [square],
-    )(*blocks)
+    def halves(pairs):
+        return [shape((8 * pairs * HALF, width), f32), shape((8 * pairs * HALF, width), bf16)]
+
+    early = call(functools.partial(early_kernel, depth), [VMEM] * 3, halves(EARLY), [square])(
+        blocks[0], blocks[3], blocks[4]
+    )
+    keep, send = call(functools.partial(late_kernel, depth), [VMEM] * 7, halves(len(PAIRS)), [square])(*blocks, *early)
     one, two, three, four, own = call(
         core_sum_kernel, [VMEM] * 2,
         [shape((n * SIZE, width), t) for n, t in ((2, bf16), (2, f32), (2, bf16), (1, bf16), (1, f32))],
@@ -214,7 +222,9 @@
     own = call(functools.partial(own_kernel, depth), [VMEM] * 6, [shape((depth, width), f32)])(*blocks, whole)[0]
 
     back = [send_home(parts[k - 1], HELD[k]) for k in (4, 3, 2, 1)]
-    return call(total_kernel, [VMEM] * 5, shape((depth, width), f32))(own, *back).T
+    for part in back:
+        own = own + part.astype(f32)
+    return own.T
 
 
 def solution(mesh):

time: 87 us -> 86.5 us (level)
  other arithmetic: 0 us -> 0.97 us
    transpose x0 -> x1, other arithmetic: none -> 0.97 us  [body(): return own.T]
  transfers between devices with their start and end apart: 22 -> 22, of which waited for: 14 -> 14; matrix products, arithmetic and copies ran while one was open for 0% -> 0% of each run, Pallas kernels for 1% -> 2%
where the time goes in v1:
time: 86.5 us; the launch traced here: 86.4 us
  starting transfers between devices  44.7 us (52%)
  waiting for transfers between devices  35.4 us (41%)
  Pallas kernels  3.62 us (4%)
  other arithmetic  0.97 us (1%)
  local copies, waits for them, and re-layouts  0.96 us (1%)
    ppermute x8, waiting for transfers between devices, send_home(): return lax.ppermute(array, 'occ', [(i, (i + by) % 16) for i in range(16)])  20.2 us
    ppermute x8, starting transfers between devices, send_home(): return lax.ppermute(array, 'occ', [(i, (i + by) % 16) for i in range(16)])  17.7 us
    ppermute x8, starting transfers between devices, along_z(): return lax.ppermute(array, 'aux', [(i, target(i)) for i in range(16)])  15.2 us
    ppermute x6, starting transfers between devices, sibling(): return lax.ppermute(array, 'aux', [(i, i ^ 1) for i in range(16)])  11.8 us
    ppermute x8, waiting for transfers between devices, along_z(): return lax.ppermute(array, 'aux', [(i, target(i)) for i in range(16)])  11.3 us
    ppermute x6, waiting for transfers between devices, sibling(): return lax.ppermute(array, 'aux', [(i, i ^ 1) for i in range(16)])  4 us
  transfers between devices with their start and end apart: 22, of which 14 were waited for; matrix products, arithmetic and copies ran while one was open for 0% of the time, Pallas kernels for 2%

profile of v1, /device:TPU:1, one launch (start us, length us, event | category | flops | bytes accessed | tf_op | source)
XLA Modules:
  0.0 86.4 jit_solution(17665137553352567027)
XLA Ops:
  1.6 4.4 %collective-permute-start.3 = (bf16[592,256]{1,0:T(8,128)(2,1)S(1)}, bf16[592,256]{1,0:T(8,128)(2,1)S(1)}, u32[]{:S(2)}, u32[]{:S(2)}) collective-permute-start(bf16[592,256]{1,0:T(8,128)(2,1)S(1)} %shard_map.37.own_ref.refs_0_), channel_id=1, source_target_pairs={{0,112},{16,128},{32,144},{48,160},{64,176},{80,192},{96,208},{112... | collective-permute-start | bytes 909320 | tf_op jit(solution)/shard_map/ppermute | solution.py:22
  7.8 3.3 %collective-permute-start = (bf16[592,256]{1,0:T(8,128)(2,1)S(1)}, bf16[592,256]{1,0:T(8,128)(2,1)S(1)}, u32[]{:S(2)}, u32[]{:S(2)}) collective-permute-start(bf16[592,256]{1,0:T(8,128)(2,1)S(1)} %shard_map.37.own_ref.refs_0_), channel_id=1, source_target_pairs={{0,240},{16,0},{32,16},{48,32},{64,48},{80,64},{96,80},{112,96},{1... | collective-permute-start | bytes 909320 | tf_op jit(solution)/shard_map/ppermute | solution.py:22
  11.9 5.1 %collective-permute-done.2.third_ref.refs_3_ = bf16[592,256]{1,0:T(8,128)(2,1)S(1)} collective-permute-done((bf16[592,256]{1,0:T(8,128)(2,1)S(1)}, bf16[592,256]{1,0:T(8,128)(2,1)S(1)}, u32[]{:S(2)}, u32[]{:S(2)}) %collective-permute-start.2) | collective-permute-done | bytes 303136 | tf_op jit(solution)/shard_map/ppermute | solution.py:22
  17.7 2.3 %collective-permute-done.1.refs_2_ = bf16[592,256]{1,0:T(8,128)(2,1)S(1)} collective-permute-done((bf16[592,256]{1,0:T(8,128)(2,1)S(1)}, bf16[592,256]{1,0:T(8,128)(2,1)S(1)}, u32[]{:S(2)}, u32[]{:S(2)}) %collective-permute-start.1) | collective-permute-done | bytes 303136 | tf_op jit(solution)/shard_map/ppermute | solution.py:22
  20.8 1.4 %collective-permute-start.4 = (bf16[1152,256]{1,0:T(8,128)(2,1)S(1)}, bf16[1152,256]{1,0:T(8,128)(2,1)S(1)}, u32[]{:S(2)}, u32[]{:S(2)}) collective-permute-start(bf16[1152,256]{1,0:T(8,128)(2,1)S(1)} %get-tuple-element.24), channel_id=1, source_target_pairs={{0,1},{1,0},{2,3},{3,2},{4,5},{5,4},{6,7},{7,6},{8,9},{9,8},{10,11... | collective-permute-start | bytes 1769480 | tf_op jit(solution)/shard_map/ppermute | solution.py:33
  22.3 1.6 %collective-permute-done.4.got_ref = bf16[1152,256]{1,0:T(8,128)(2,1)S(1)} collective-permute-done((bf16[1152,256]{1,0:T(8,128)(2,1)S(1)}, bf16[1152,256]{1,0:T(8,128)(2,1)S(1)}, u32[]{:S(2)}, u32[]{:S(2)}) %collective-permute-start.4) | collective-permute-done | bytes 589856 | tf_op jit(solution)/shard_map/ppermute | solution.py:33
  24.0 5.7 %collective-permute-start.6 = (bf16[288,256]{1,0:T(8,128)(2,1)S(1)}, bf16[288,256]{1,0:T(8,128)(2,1)S(1)}, u32[]{:S(2)}, u32[]{:S(2)}) collective-permute-start(bf16[288,256]{1,0:T(8,128)(2,1)S(1)} %get-tuple-element.28), channel_id=1, source_target_pairs={{0,2},{1,15},{2,4},{3,1},{4,6},{5,3},{6,8},{7,5},{8,10},{9,7},{10,... | collective-permute-start | bytes 442376 | tf_op jit(solution)/shard_map/ppermute | solution.py:29
  31.5 2.5 %collective-permute-done.7.four_ref = bf16[144,256]{1,0:T(8,128)(2,1)S(1)} collective-permute-done((bf16[144,256]{1,0:T(8,128)(2,1)S(1)}, bf16[144,256]{1,0:T(8,128)(2,1)S(1)}, u32[]{:S(2)}, u32[]{:S(2)}) %collective-permute-start.7) | collective-permute-done | bytes 73760 | tf_op jit(solution)/shard_map/ppermute | solution.py:29
  34.1 3.2 %collective-permute-start.8 = (bf16[288,256]{1,0:T(8,128)(2,1)S(1)}, bf16[288,256]{1,0:T(8,128)(2,1)S(1)}, u32[]{:S(2)}, u32[]{:S(2)}) collective-permute-start(bf16[288,256]{1,0:T(8,128)(2,1)S(1)} %shard_map.41), channel_id=1, source_target_pairs={{0,4},{1,13},{2,6},{3,15},{4,8},{5,1},{6,10},{7,3},{8,12},{9,5},{1... | collective-permute-start | bytes 442376 | tf_op jit(solution)/shard_map/ppermute | solution.py:29
  37.3 3.4 %collective-permute-done.8.two_ref = bf16[288,256]{1,0:T(8,128)(2,1)S(1)} collective-permute-done((bf16[288,256]{1,0:T(8,128)(2,1)S(1)}, bf16[288,256]{1,0:T(8,128)(2,1)S(1)}, u32[]{:S(2)}, u32[]{:S(2)}) %collective-permute-start.8) | collective-permute-done | bytes 147488 | tf_op jit(solution)/shard_map/ppermute | solution.py:29
  40.7 4.5 %collective-permute-start.9 = (f32[288,256]{1,0:T(8,128)S(1)}, f32[288,256]{1,0:T(8,128)S(1)}, u32[]{:S(2)}, u32[]{:S(2)}) collective-permute-start(f32[288,256]{1,0:T(8,128)S(1)} %shard_map.42.refs_5_), channel_id=1, source_target_pairs={{0,1},{1,0},{2,3},{3,2},{4,5},{5,4},{6,7},{7,6},{8,9},{9,8},{10,11... | collective-permute-start | bytes 884744 | tf_op jit(solution)/shard_map/ppermute | solution.py:33
  46.6 1.7 %collective-permute-start.10 = (bf16[288,256]{1,0:T(8,128)(2,1)S(1)}, bf16[288,256]{1,0:T(8,128)(2,1)S(1)}, u32[]{:S(2)}, u32[]{:S(2)}) collective-permute-start(bf16[288,256]{1,0:T(8,128)(2,1)S(1)} %shard_map.44.refs_5_), channel_id=1, source_target_pairs={{0,2},{1,15},{2,4},{3,1},{4,6},{5,3},{6,8},{7,5},{8,10},{9,7},{10,... | collective-permute-start | bytes 442376 | tf_op jit(solution)/shard_map/ppermute | solution.py:29
  48.3 3.5 %collective-permute-done.11.refs_7_ = bf16[288,256]{1,0:T(8,128)(2,1)S(1)} collective-permute-done((bf16[288,256]{1,0:T(8,128)(2,1)S(1)}, bf16[288,256]{1,0:T(8,128)(2,1)S(1)}, u32[]{:S(2)}, u32[]{:S(2)}) %collective-permute-start.11) | collective-permute-done | bytes 147488 | tf_op jit(solution)/shard_map/ppermute | solution.py:29
  51.9 2.6 %collective-permute-start.12 = (bf16[288,256]{1,0:T(8,128)(2,1)S(1)}, bf16[288,256]{1,0:T(8,128)(2,1)S(1)}, u32[]{:S(2)}, u32[]{:S(2)}) collective-permute-start(bf16[288,256]{1,0:T(8,128)(2,1)S(1)} %collective-permute-done.11.refs_7_), channel_id=1, source_target_pairs={{0,2},{1,15},{2,4},{3,1},{4,6},{5,3},{6,8},{7,5},{8,10},{9,7},{10,... | collective-permute-start | bytes 442376 | tf_op jit(solution)/shard_map/ppermute | solution.py:29
  55.5 1.8 %collective-permute-done.12.refs_8_ = bf16[288,256]{1,0:T(8,128)(2,1)S(1)} collective-permute-done((bf16[288,256]{1,0:T(8,128)(2,1)S(1)}, bf16[288,256]{1,0:T(8,128)(2,1)S(1)}, u32[]{:S(2)}, u32[]{:S(2)}) %collective-permute-start.12) | collective-permute-done | bytes 147488 | tf_op jit(solution)/shard_map/ppermute | solution.py:29
  57.3 4.8 %collective-permute-start.16 = (bf16[288,256]{1,0:T(8,128)(2,1)S(1)}, bf16[288,256]{1,0:T(8,128)(2,1)S(1)}, u32[]{:S(2)}, u32[]{:S(2)}) collective-permute-start(bf16[288,256]{1,0:T(8,128)(2,1)S(1)} %collective-permute-done.12.refs_8_), channel_id=1, source_target_pairs={{0,1},{1,0},{2,3},{3,2},{4,5},{5,4},{6,7},{7,6},{8,9},{9,8},{10,11... | collective-permute-start | bytes 442376 | tf_op jit(solution)/shard_map/ppermute | solution.py:33
  62.2 1.3 %collective-permute-done.17.refs_13_ = bf16[144,256]{1,0:T(8,128)(2,1)S(1)} collective-permute-done((bf16[144,256]{1,0:T(8,128)(2,1)S(1)}, bf16[144,256]{1,0:T(8,128)(2,1)S(1)}, u32[]{:S(2)}, u32[]{:S(2)}) %collective-permute-start.17) | collective-permute-done | bytes 73760 | tf_op jit(solution)/shard_map/ppermute | solution.py:33
  64.6 3.6 %collective-permute-start.18 = (bf16[576,256]{1,0:T(8,128)(2,1)S(1)}, bf16[576,256]{1,0:T(8,128)(2,1)S(1)}, u32[]{:S(2)}, u32[]{:S(2)}) collective-permute-start(bf16[576,256]{1,0:T(8,128)(2,1)S(1)} %get-tuple-element.33), channel_id=1, source_target_pairs={{0,144},{16,160},{32,176},{48,192},{64,208},{80,224},{96,240},{112... | collective-permute-start | bytes 884744 | tf_op jit(solution)/shard_map/ppermute | solution.py:22
  68.6 3.0 %collective-permute-start.20 = (bf16[576,256]{1,0:T(8,128)(2,1)S(1)}, bf16[576,256]{1,0:T(8,128)(2,1)S(1)}, u32[]{:S(2)}, u32[]{:S(2)}) collective-permute-start(bf16[576,256]{1,0:T(8,128)(2,1)S(1)} %get-tuple-element.35), channel_id=1, source_target_pairs={{0,192},{16,208},{32,224},{48,240},{64,0},{80,16},{96,32},{112,48}... | collective-permute-start | bytes 884744 | tf_op jit(solution)/shard_map/ppermute | solution.py:22
  71.6 1.2 %collective-permute-start.21 = (bf16[576,256]{1,0:T(8,128)(2,1)S(1)}, bf16[576,256]{1,0:T(8,128)(2,1)S(1)}, u32[]{:S(2)}, u32[]{:S(2)}) collective-permute-start(bf16[576,256]{1,0:T(8,128)(2,1)S(1)} %get-tuple-element.36), channel_id=1, source_target_pairs={{0,16},{16,32},{32,48},{48,64},{64,80},{80,96},{96,112},{112,128},... | collective-permute-start | bytes 884744 | tf_op jit(solution)/shard_map/ppermute | solution.py:22
  73.4 3.6 %collective-permute-done.18 = bf16[576,256]{1,0:T(8,128)(2,1)S(1)} collective-permute-done((bf16[576,256]{1,0:T(8,128)(2,1)S(1)}, bf16[576,256]{1,0:T(8,128)(2,1)S(1)}, u32[]{:S(2)}, u32[]{:S(2)}) %collective-permute-start.18) | collective-permute-done | bytes 294944 | tf_op jit(solution)/shard_map/ppermute | solution.py:22
  77.0 4.4 %collective-permute-done.19 = bf16[576,256]{1,0:T(8,128)(2,1)S(1)} collective-permute-done((bf16[576,256]{1,0:T(8,128)(2,1)S(1)}, bf16[576,256]{1,0:T(8,128)(2,1)S(1)}, u32[]{:S(2)}, u32[]{:S(2)}) %collective-permute-start.19) | collective-permute-done | bytes 294944 | tf_op jit(solution)/shard_map/ppermute | solution.py:22
  81.4 1.3 %collective-permute-done.20 = bf16[576,256]{1,0:T(8,128)(2,1)S(1)} collective-permute-done((bf16[576,256]{1,0:T(8,128)(2,1)S(1)}, bf16[576,256]{1,0:T(8,128)(2,1)S(1)}, u32[]{:S(2)}, u32[]{:S(2)}) %collective-permute-start.20) | collective-permute-done | bytes 294944 | tf_op jit(solution)/shard_map/ppermute | solution.py:22
  82.7 2.7 %collective-permute-done.21 = bf16[576,256]{1,0:T(8,128)(2,1)S(1)} collective-permute-done((bf16[576,256]{1,0:T(8,128)(2,1)S(1)}, bf16[576,256]{1,0:T(8,128)(2,1)S(1)}, u32[]{:S(2)}, u32[]{:S(2)}) %collective-permute-start.21) | collective-permute-done | bytes 294944 | tf_op jit(solution)/shard_map/ppermute | solution.py:22
  (36 shorter events, 12.7 us)
Async XLA Ops:
  0.7 1.0 %copy-start = (bf16[256,576]{0,1:T(8,128)(2,1)S(1)}, bf16[256,576]{0,1:T(8,128)(2,1)}, u32[]{:S(2)}) copy-start(bf16[256,576]{0,1:T(8,128)(2,1)} %param.3) | copy-start | bytes 884740
  1.6 10.3 %collective-permute-start.3 = (bf16[592,256]{1,0:T(8,128)(2,1)S(1)}, bf16[592,256]{1,0:T(8,128)(2,1)S(1)}, u32[]{:S(2)}, u32[]{:S(2)}) collective-permute-start(bf16[592,256]{1,0:T(8,128)(2,1)S(1)} %shard_map.37.own_ref.refs_0_), channel_id=1, source_target_pairs={{0,112},{16,128},{32,144},{48,160},{64,176},{80,192},{96,208},{112... | collective-permute-start | bytes 909320 | tf_op jit(solution)/shard_map/ppermute | solution.py:22
  6.0 11.0 %collective-permute-start.2 = (bf16[592,256]{1,0:T(8,128)(2,1)S(1)}, bf16[592,256]{1,0:T(8,128)(2,1)S(1)}, u32[]{:S(2)}, u32[]{:S(2)}) collective-permute-start(bf16[592,256]{1,0:T(8,128)(2,1)S(1)} %shard_map.37.own_ref.refs_0_), channel_id=1, source_target_pairs={{0,208},{16,224},{32,240},{48,0},{64,16},{80,32},{96,48},{112,64},... | collective-permute-start | bytes 909320 | tf_op jit(solution)/shard_map/ppermute | solution.py:22
  7.1 12.8 %collective-permute-start.1 = (bf16[592,256]{1,0:T(8,128)(2,1)S(1)}, bf16[592,256]{1,0:T(8,128)(2,1)S(1)}, u32[]{:S(2)}, u32[]{:S(2)}) collective-permute-start(bf16[592,256]{1,0:T(8,128)(2,1)S(1)} %shard_map.37.own_ref.refs_0_), channel_id=1, source_target_pairs={{0,64},{16,80},{32,96},{48,112},{64,128},{80,144},{96,160},{112,17... | collective-permute-start | bytes 909320 | tf_op jit(solution)/shard_map/ppermute | solution.py:22
  7.8 12.1 %collective-permute-start = (bf16[592,256]{1,0:T(8,128)(2,1)S(1)}, bf16[592,256]{1,0:T(8,128)(2,1)S(1)}, u32[]{:S(2)}, u32[]{:S(2)}) collective-permute-start(bf16[592,256]{1,0:T(8,128)(2,1)S(1)} %shard_map.37.own_ref.refs_0_), channel_id=1, source_target_pairs={{0,240},{16,0},{32,16},{48,32},{64,48},{80,64},{96,80},{112,96},{1... | collective-permute-start | bytes 909320 | tf_op jit(solution)/shard_map/ppermute | solution.py:22
  20.8 3.1 %collective-permute-start.4 = (bf16[1152,256]{1,0:T(8,128)(2,1)S(1)}, bf16[1152,256]{1,0:T(8,128)(2,1)S(1)}, u32[]{:S(2)}, u32[]{:S(2)}) collective-permute-start(bf16[1152,256]{1,0:T(8,128)(2,1)S(1)} %get-tuple-element.24), channel_id=1, source_target_pairs={{0,1},{1,0},{2,3},{3,2},{4,5},{5,4},{6,7},{7,6},{8,9},{9,8},{10,11... | collective-permute-start | bytes 1769480 | tf_op jit(solution)/shard_map/ppermute | solution.py:33
  23.9 21.4 %copy-start.1 = (f32[256]{0:T(256)S(1)}, f32[256]{0:T(256)}, u32[]{:S(2)}) copy-start(f32[256]{0:T(256)} %param.5) | copy-start | bytes 3076
  24.0 10.1 %collective-permute-start.6 = (bf16[288,256]{1,0:T(8,128)(2,1)S(1)}, bf16[288,256]{1,0:T(8,128)(2,1)S(1)}, u32[]{:S(2)}, u32[]{:S(2)}) collective-permute-start(bf16[288,256]{1,0:T(8,128)(2,1)S(1)} %get-tuple-element.28), channel_id=1, source_target_pairs={{0,2},{1,15},{2,4},{3,1},{4,6},{5,3},{6,8},{7,5},{8,10},{9,7},{10,... | collective-permute-start | bytes 442376 | tf_op jit(solution)/shard_map/ppermute | solution.py:29
  29.6 4.4 %collective-permute-start.7 = (bf16[144,256]{1,0:T(8,128)(2,1)S(1)}, bf16[144,256]{1,0:T(8,128)(2,1)S(1)}, u32[]{:S(2)}, u32[]{:S(2)}) collective-permute-start(bf16[144,256]{1,0:T(8,128)(2,1)S(1)} %get-tuple-element.29), channel_id=1, source_target_pairs={{0,4},{1,13},{2,6},{3,15},{4,8},{5,1},{6,10},{7,3},{8,12},{9,5},{1... | collective-permute-start | bytes 221192 | tf_op jit(solution)/shard_map/ppermute | solution.py:29
  30.8 6.5 %collective-permute-start.5 = (bf16[288,256]{1,0:T(8,128)(2,1)S(1)}, bf16[288,256]{1,0:T(8,128)(2,1)S(1)}, u32[]{:S(2)}, u32[]{:S(2)}) collective-permute-start(bf16[288,256]{1,0:T(8,128)(2,1)S(1)} %get-tuple-element.26), channel_id=1, source_target_pairs={{0,2},{1,15},{2,4},{3,1},{4,6},{5,3},{6,8},{7,5},{8,10},{9,7},{10,... | collective-permute-start | bytes 442376 | tf_op jit(solution)/shard_map/ppermute | solution.py:29
  34.1 6.6 %collective-permute-start.8 = (bf16[288,256]{1,0:T(8,128)(2,1)S(1)}, bf16[288,256]{1,0:T(8,128)(2,1)S(1)}, u32[]{:S(2)}, u32[]{:S(2)}) collective-permute-start(bf16[288,256]{1,0:T(8,128)(2,1)S(1)} %shard_map.41), channel_id=1, source_target_pairs={{0,4},{1,13},{2,6},{3,15},{4,8},{5,1},{6,10},{7,3},{8,12},{9,5},{1... | collective-permute-start | bytes 442376 | tf_op jit(solution)/shard_map/ppermute | solution.py:29
  40.7 5.8 %collective-permute-start.9 = (f32[288,256]{1,0:T(8,128)S(1)}, f32[288,256]{1,0:T(8,128)S(1)}, u32[]{:S(2)}, u32[]{:S(2)}) collective-permute-start(f32[288,256]{1,0:T(8,128)S(1)} %shard_map.42.refs_5_), channel_id=1, source_target_pairs={{0,1},{1,0},{2,3},{3,2},{4,5},{5,4},{6,7},{7,6},{8,9},{9,8},{10,11... | collective-permute-start | bytes 884744 | tf_op jit(solution)/shard_map/ppermute | solution.py:33
  46.6 5.3 %collective-permute-start.11 = (bf16[288,256]{1,0:T(8,128)(2,1)S(1)}, bf16[288,256]{1,0:T(8,128)(2,1)S(1)}, u32[]{:S(2)}, u32[]{:S(2)}) collective-permute-start(bf16[288,256]{1,0:T(8,128)(2,1)S(1)} %shard_map.44.refs_5_), channel_id=1, source_target_pairs={{0,4},{1,13},{2,6},{3,15},{4,8},{5,1},{6,10},{7,3},{8,12},{9,5},{1... | collective-permute-start | bytes 442376 | tf_op jit(solution)/shard_map/ppermute | solution.py:29
  46.6 8.7 %collective-permute-start.10 = (bf16[288,256]{1,0:T(8,128)(2,1)S(1)}, bf16[288,256]{1,0:T(8,128)(2,1)S(1)}, u32[]{:S(2)}, u32[]{:S(2)}) collective-permute-start(bf16[288,256]{1,0:T(8,128)(2,1)S(1)} %shard_map.44.refs_5_), channel_id=1, source_target_pairs={{0,2},{1,15},{2,4},{3,1},{4,6},{5,3},{6,8},{7,5},{8,10},{9,7},{10,... | collective-permute-start | bytes 442376 | tf_op jit(solution)/shard_map/ppermute | solution.py:29
  51.9 5.5 %collective-permute-start.12 = (bf16[288,256]{1,0:T(8,128)(2,1)S(1)}, bf16[288,256]{1,0:T(8,128)(2,1)S(1)}, u32[]{:S(2)}, u32[]{:S(2)}) collective-permute-start(bf16[288,256]{1,0:T(8,128)(2,1)S(1)} %collective-permute-done.11.refs_7_), channel_id=1, source_target_pairs={{0,2},{1,15},{2,4},{3,1},{4,6},{5,3},{6,8},{7,5},{8,10},{9,7},{10,... | collective-permute-start | bytes 442376 | tf_op jit(solution)/shard_map/ppermute | solution.py:29
  54.5 7.7 %collective-permute-start.13 = (bf16[144,256]{1,0:T(8,128)(2,1)S(1)}, bf16[144,256]{1,0:T(8,128)(2,1)S(1)}, u32[]{:S(2)}, u32[]{:S(2)}) collective-permute-start(bf16[144,256]{1,0:T(8,128)(2,1)S(1)} %slice.4), channel_id=1, source_target_pairs={{0,4},{1,13},{2,6},{3,15},{4,8},{5,1},{6,10},{7,3},{8,12},{9,5},{1... | collective-permute-start | bytes 221192 | tf_op jit(solution)/shard_map/ppermute | solution.py:29
  54.5 8.9 %collective-permute-start.15 = (bf16[288,256]{1,0:T(8,128)(2,1)S(1)}, bf16[288,256]{1,0:T(8,128)(2,1)S(1)}, u32[]{:S(2)}, u32[]{:S(2)}) collective-permute-start(bf16[288,256]{1,0:T(8,128)(2,1)S(1)} %collective-permute-done.11.refs_7_), channel_id=1, source_target_pairs={{0,1},{1,0},{2,3},{3,2},{4,5},{5,4},{6,7},{7,6},{8,9},{9,8},{10,11... | collective-permute-start | bytes 442376 | tf_op jit(solution)/shard_map/ppermute | solution.py:33
  55.4 8.0 %collective-permute-start.14 = (bf16[288,256]{1,0:T(8,128)(2,1)S(1)}, bf16[288,256]{1,0:T(8,128)(2,1)S(1)}, u32[]{:S(2)}, u32[]{:S(2)}) collective-permute-start(bf16[288,256]{1,0:T(8,128)(2,1)S(1)} %collective-permute-done.10.refs_6_), channel_id=1, source_target_pairs={{0,1},{1,0},{2,3},{3,2},{4,5},{5,4},{6,7},{7,6},{8,9},{9,8},{10,11... | collective-permute-start | bytes 442376 | tf_op jit(solution)/shard_map/ppermute | solution.py:33
  57.3 6.1 %collective-permute-start.16 = (bf16[288,256]{1,0:T(8,128)(2,1)S(1)}, bf16[288,256]{1,0:T(8,128)(2,1)S(1)}, u32[]{:S(2)}, u32[]{:S(2)}) collective-permute-start(bf16[288,256]{1,0:T(8,128)(2,1)S(1)} %collective-permute-done.12.refs_8_), channel_id=1, source_target_pairs={{0,1},{1,0},{2,3},{3,2},{4,5},{5,4},{6,7},{7,6},{8,9},{9,8},{10,11... | collective-permute-start | bytes 442376 | tf_op jit(solution)/shard_map/ppermute | solution.py:33
  62.1 1.3 %collective-permute-start.17 = (bf16[144,256]{1,0:T(8,128)(2,1)S(1)}, bf16[144,256]{1,0:T(8,128)(2,1)S(1)}, u32[]{:S(2)}, u32[]{:S(2)}) collective-permute-start(bf16[144,256]{1,0:T(8,128)(2,1)S(1)} %collective-permute-done.13.refs_9_), channel_id=1, source_target_pairs={{0,1},{1,0},{2,3},{3,2},{4,5},{5,4},{6,7},{7,6},{8,9},{9,8},{10,11... | collective-permute-start | bytes 221192 | tf_op jit(solution)/shard_map/ppermute | solution.py:33
  64.6 12.4 %collective-permute-start.18 = (bf16[576,256]{1,0:T(8,128)(2,1)S(1)}, bf16[576,256]{1,0:T(8,128)(2,1)S(1)}, u32[]{:S(2)}, u32[]{:S(2)}) collective-permute-start(bf16[576,256]{1,0:T(8,128)(2,1)S(1)} %get-tuple-element.33), channel_id=1, source_target_pairs={{0,144},{16,160},{32,176},{48,192},{64,208},{80,224},{96,240},{112... | collective-permute-start | bytes 884744 | tf_op jit(solution)/shard_map/ppermute | solution.py:22
  68.2 13.1 %collective-permute-start.19 = (bf16[576,256]{1,0:T(8,128)(2,1)S(1)}, bf16[576,256]{1,0:T(8,128)(2,1)S(1)}, u32[]{:S(2)}, u32[]{:S(2)}) collective-permute-start(bf16[576,256]{1,0:T(8,128)(2,1)S(1)} %get-tuple-element.34), channel_id=1, source_target_pairs={{0,48},{16,64},{32,80},{48,96},{64,112},{80,128},{96,144},{112,160... | collective-permute-start | bytes 884744 | tf_op jit(solution)/shard_map/ppermute | solution.py:22
  68.6 14.0 %collective-permute-start.20 = (bf16[576,256]{1,0:T(8,128)(2,1)S(1)}, bf16[576,256]{1,0:T(8,128)(2,1)S(1)}, u32[]{:S(2)}, u32[]{:S(2)}) collective-permute-start(bf16[576,256]{1,0:T(8,128)(2,1)S(1)} %get-tuple-element.35), channel_id=1, source_target_pairs={{0,192},{16,208},{32,224},{48,240},{64,0},{80,16},{96,32},{112,48}... | collective-permute-start | bytes 884744 | tf_op jit(solution)/shard_map/ppermute | solution.py:22
  71.6 13.8 %collective-permute-start.21 = (bf16[576,256]{1,0:T(8,128)(2,1)S(1)}, bf16[576,256]{1,0:T(8,128)(2,1)S(1)}, u32[]{:S(2)}, u32[]{:S(2)}) collective-permute-start(bf16[576,256]{1,0:T(8,128)(2,1)S(1)} %get-tuple-element.36), channel_id=1, source_target_pairs={{0,16},{16,32},{32,48},{48,64},{64,80},{80,96},{96,112},{112,128},... | collective-permute-start | bytes 884744 | tf_op jit(solution)/shard_map/ppermute | solution.py:22

commit v2 on v1

--- a/solution.py
+++ b/solution.py
@@ -221,7 +221,7 @@
     *parts, whole = parts
     own = call(functools.partial(own_kernel, depth), [VMEM] * 6, [shape((depth, width), f32)])(*blocks, whole)[0]
 
-    back = [send_home(parts[k - 1], HELD[k]) for k in (4, 3, 2, 1)]
+    back = [send_home(parts[k - 1], HELD[k]) for k in (4, 3, 1, 2)]
     for part in back:
         own = own + part.astype(f32)
     return own.T

time: 86.5 us -> 87.2 us (level)
  transfers between devices with their start and end apart: 22 -> 22, of which waited for: 14 -> 13; matrix products, arithmetic and copies ran while one was open for 0% -> 0% of each run, Pallas kernels for 2% -> 2%
where the time goes in v2:
time: 87.2 us; the launch traced here: 87.1 us
  starting transfers between devices  44.7 us (51%)
  waiting for transfers between devices  36.1 us (41%)
  Pallas kernels  3.62 us (4%)
  other arithmetic  0.97 us (1%)
  local copies, waits for them, and re-layouts  0.96 us (1%)
    ppermute x8, waiting for transfers between devices, send_home(): return lax.ppermute(array, 'occ', [(i, (i + by) % 16) for i in range(16)])  20.8 us
    ppermute x8, starting transfers between devices, send_home(): return lax.ppermute(array, 'occ', [(i, (i + by) % 16) for i in range(16)])  17.7 us
    ppermute x8, starting transfers between devices, along_z(): return lax.ppermute(array, 'aux', [(i, target(i)) for i in range(16)])  15.2 us
    ppermute x6, starting transfers between devices, sibling(): return lax.ppermute(array, 'aux', [(i, i ^ 1) for i in range(16)])  11.8 us
    ppermute x8, waiting for transfers between devices, along_z(): return lax.ppermute(array, 'aux', [(i, target(i)) for i in range(16)])  11.3 us
    ppermute x6, waiting for transfers between devices, sibling(): return lax.ppermute(array, 'aux', [(i, i ^ 1) for i in range(16)])  4 us
  transfers between devices with their start and end apart: 22, of which 13 were waited for; matrix products, arithmetic and copies ran while one was open for 0% of the time, Pallas kernels for 2%

profile of v2, /device:TPU:1, one launch (start us, length us, event | category | flops | bytes accessed | tf_op | source)
XLA Modules:
  0.0 87.1 jit_solution(6355178271855589153)
XLA Ops:
  1.6 4.4 %collective-permute-start.3 = (bf16[592,256]{1,0:T(8,128)(2,1)S(1)}, bf16[592,256]{1,0:T(8,128)(2,1)S(1)}, u32[]{:S(2)}, u32[]{:S(2)}) collective-permute-start(bf16[592,256]{1,0:T(8,128)(2,1)S(1)} %shard_map.37.own_ref.refs_0_), channel_id=1, source_target_pairs={{0,112},{16,128},{32,144},{48,160},{64,176},{80,192},{96,208},{112... | collective-permute-start | bytes 909320 | tf_op jit(solution)/shard_map/ppermute | solution.py:22
  7.8 3.3 %collective-permute-start = (bf16[592,256]{1,0:T(8,128)(2,1)S(1)}, bf16[592,256]{1,0:T(8,128)(2,1)S(1)}, u32[]{:S(2)}, u32[]{:S(2)}) collective-permute-start(bf16[592,256]{1,0:T(8,128)(2,1)S(1)} %shard_map.37.own_ref.refs_0_), channel_id=1, source_target_pairs={{0,240},{16,0},{32,16},{48,32},{64,48},{80,64},{96,80},{112,96},{1... | collective-permute-start | bytes 909320 | tf_op jit(solution)/shard_map/ppermute | solution.py:22
  11.9 5.1 %collective-permute-done.2.third_ref.refs_3_ = bf16[592,256]{1,0:T(8,128)(2,1)S(1)} collective-permute-done((bf16[592,256]{1,0:T(8,128)(2,1)S(1)}, bf16[592,256]{1,0:T(8,128)(2,1)S(1)}, u32[]{:S(2)}, u32[]{:S(2)}) %collective-permute-start.2) | collective-permute-done | bytes 303136 | tf_op jit(solution)/shard_map/ppermute | solution.py:22
  17.7 2.3 %collective-permute-done.1.refs_2_ = bf16[592,256]{1,0:T(8,128)(2,1)S(1)} collective-permute-done((bf16[592,256]{1,0:T(8,128)(2,1)S(1)}, bf16[592,256]{1,0:T(8,128)(2,1)S(1)}, u32[]{:S(2)}, u32[]{:S(2)}) %collective-permute-start.1) | collective-permute-done | bytes 303136 | tf_op jit(solution)/shard_map/ppermute | solution.py:22
  20.8 1.4 %collective-permute-start.4 = (bf16[1152,256]{1,0:T(8,128)(2,1)S(1)}, bf16[1152,256]{1,0:T(8,128)(2,1)S(1)}, u32[]{:S(2)}, u32[]{:S(2)}) collective-permute-start(bf16[1152,256]{1,0:T(8,128)(2,1)S(1)} %get-tuple-element.24), channel_id=1, source_target_pairs={{0,1},{1,0},{2,3},{3,2},{4,5},{5,4},{6,7},{7,6},{8,9},{9,8},{10,11... | collective-permute-start | bytes 1769480 | tf_op jit(solution)/shard_map/ppermute | solution.py:33
  22.3 1.6 %collective-permute-done.4.got_ref = bf16[1152,256]{1,0:T(8,128)(2,1)S(1)} collective-permute-done((bf16[1152,256]{1,0:T(8,128)(2,1)S(1)}, bf16[1152,256]{1,0:T(8,128)(2,1)S(1)}, u32[]{:S(2)}, u32[]{:S(2)}) %collective-permute-start.4) | collective-permute-done | bytes 589856 | tf_op jit(solution)/shard_map/ppermute | solution.py:33
  24.0 5.7 %collective-permute-start.6 = (bf16[288,256]{1,0:T(8,128)(2,1)S(1)}, bf16[288,256]{1,0:T(8,128)(2,1)S(1)}, u32[]{:S(2)}, u32[]{:S(2)}) collective-permute-start(bf16[288,256]{1,0:T(8,128)(2,1)S(1)} %get-tuple-element.28), channel_id=1, source_target_pairs={{0,2},{1,15},{2,4},{3,1},{4,6},{5,3},{6,8},{7,5},{8,10},{9,7},{10,... | collective-permute-start | bytes 442376 | tf_op jit(solution)/shard_map/ppermute | solution.py:29
  29.6 1.2 %collective-permute-start.7 = (bf16[144,256]{1,0:T(8,128)(2,1)S(1)}, bf16[144,256]{1,0:T(8,128)(2,1)S(1)}, u32[]{:S(2)}, u32[]{:S(2)}) collective-permute-start(bf16[144,256]{1,0:T(8,128)(2,1)S(1)} %get-tuple-element.29), channel_id=1, source_target_pairs={{0,4},{1,13},{2,6},{3,15},{4,8},{5,1},{6,10},{7,3},{8,12},{9,5},{1... | collective-permute-start | bytes 221192 | tf_op jit(solution)/shard_map/ppermute | solution.py:29
  31.5 2.5 %collective-permute-done.7.four_ref = bf16[144,256]{1,0:T(8,128)(2,1)S(1)} collective-permute-done((bf16[144,256]{1,0:T(8,128)(2,1)S(1)}, bf16[144,256]{1,0:T(8,128)(2,1)S(1)}, u32[]{:S(2)}, u32[]{:S(2)}) %collective-permute-start.7) | collective-permute-done | bytes 73760 | tf_op jit(solution)/shard_map/ppermute | solution.py:29
  34.1 3.2 %collective-permute-start.8 = (bf16[288,256]{1,0:T(8,128)(2,1)S(1)}, bf16[288,256]{1,0:T(8,128)(2,1)S(1)}, u32[]{:S(2)}, u32[]{:S(2)}) collective-permute-start(bf16[288,256]{1,0:T(8,128)(2,1)S(1)} %shard_map.41), channel_id=1, source_target_pairs={{0,4},{1,13},{2,6},{3,15},{4,8},{5,1},{6,10},{7,3},{8,12},{9,5},{1... | collective-permute-start | bytes 442376 | tf_op jit(solution)/shard_map/ppermute | solution.py:29
  37.3 3.4 %collective-permute-done.8.two_ref = bf16[288,256]{1,0:T(8,128)(2,1)S(1)} collective-permute-done((bf16[288,256]{1,0:T(8,128)(2,1)S(1)}, bf16[288,256]{1,0:T(8,128)(2,1)S(1)}, u32[]{:S(2)}, u32[]{:S(2)}) %collective-permute-start.8) | collective-permute-done | bytes 147488 | tf_op jit(solution)/shard_map/ppermute | solution.py:29
  40.7 4.5 %collective-permute-start.9 = (f32[288,256]{1,0:T(8,128)S(1)}, f32[288,256]{1,0:T(8,128)S(1)}, u32[]{:S(2)}, u32[]{:S(2)}) collective-permute-start(f32[288,256]{1,0:T(8,128)S(1)} %shard_map.42.refs_5_), channel_id=1, source_target_pairs={{0,1},{1,0},{2,3},{3,2},{4,5},{5,4},{6,7},{7,6},{8,9},{9,8},{10,11... | collective-permute-start | bytes 884744 | tf_op jit(solution)/shard_map/ppermute | solution.py:33
  46.6 1.7 %collective-permute-start.10 = (bf16[288,256]{1,0:T(8,128)(2,1)S(1)}, bf16[288,256]{1,0:T(8,128)(2,1)S(1)}, u32[]{:S(2)}, u32[]{:S(2)}) collective-permute-start(bf16[288,256]{1,0:T(8,128)(2,1)S(1)} %shard_map.44.refs_5_), channel_id=1, source_target_pairs={{0,2},{1,15},{2,4},{3,1},{4,6},{5,3},{6,8},{7,5},{8,10},{9,7},{10,... | collective-permute-start | bytes 442376 | tf_op jit(solution)/shard_map/ppermute | solution.py:29
  48.3 3.5 %collective-permute-done.11.refs_7_ = bf16[288,256]{1,0:T(8,128)(2,1)S(1)} collective-permute-done((bf16[288,256]{1,0:T(8,128)(2,1)S(1)}, bf16[288,256]{1,0:T(8,128)(2,1)S(1)}, u32[]{:S(2)}, u32[]{:S(2)}) %collective-permute-start.11) | collective-permute-done | bytes 147488 | tf_op jit(solution)/shard_map/ppermute | solution.py:29
  51.9 2.6 %collective-permute-start.12 = (bf16[288,256]{1,0:T(8,128)(2,1)S(1)}, bf16[288,256]{1,0:T(8,128)(2,1)S(1)}, u32[]{:S(2)}, u32[]{:S(2)}) collective-permute-start(bf16[288,256]{1,0:T(8,128)(2,1)S(1)} %collective-permute-done.11.refs_7_), channel_id=1, source_target_pairs={{0,2},{1,15},{2,4},{3,1},{4,6},{5,3},{6,8},{7,5},{8,10},{9,7},{10,... | collective-permute-start | bytes 442376 | tf_op jit(solution)/shard_map/ppermute | solution.py:29
  55.5 1.8 %collective-permute-done.12.refs_8_ = bf16[288,256]{1,0:T(8,128)(2,1)S(1)} collective-permute-done((bf16[288,256]{1,0:T(8,128)(2,1)S(1)}, bf16[288,256]{1,0:T(8,128)(2,1)S(1)}, u32[]{:S(2)}, u32[]{:S(2)}) %collective-permute-start.12) | collective-permute-done | bytes 147488 | tf_op jit(solution)/shard_map/ppermute | solution.py:29
  57.3 4.8 %collective-permute-start.16 = (bf16[288,256]{1,0:T(8,128)(2,1)S(1)}, bf16[288,256]{1,0:T(8,128)(2,1)S(1)}, u32[]{:S(2)}, u32[]{:S(2)}) collective-permute-start(bf16[288,256]{1,0:T(8,128)(2,1)S(1)} %collective-permute-done.12.refs_8_), channel_id=1, source_target_pairs={{0,1},{1,0},{2,3},{3,2},{4,5},{5,4},{6,7},{7,6},{8,9},{9,8},{10,11... | collective-permute-start | bytes 442376 | tf_op jit(solution)/shard_map/ppermute | solution.py:33
  62.2 1.3 %collective-permute-done.17.refs_13_ = bf16[144,256]{1,0:T(8,128)(2,1)S(1)} collective-permute-done((bf16[144,256]{1,0:T(8,128)(2,1)S(1)}, bf16[144,256]{1,0:T(8,128)(2,1)S(1)}, u32[]{:S(2)}, u32[]{:S(2)}) %collective-permute-start.17) | collective-permute-done | bytes 73760 | tf_op jit(solution)/shard_map/ppermute | solution.py:33
  63.4 1.2 %shard_map.45 = (bf16[576,256]{1,0:T(8,128)(2,1)S(1)}, bf16[576,256]{1,0:T(8,128)(2,1)S(1)}, bf16[576,256]{1,0:T(8,128)(2,1)S(1)}, bf16[576,256]{1,0:T(8,128)(2,1)S(1)}, bf16[9,256,256]{2,1,0:T(8,128)(2,1)S(1)}) custom-call(bf16[592,256]{1,0:T(8,128)(2,1)S(1)} %shard_map.37.own_ref.refs_0_, bf16[592,256]{1,0:T(8,128)(2,1)S(1)} %collective-permute-done.refs_1_, ...), custom_call_target="tpu_custom_call" | custom-call | tf_op jit(solution)/shard_map/pallas_call | solution.py:216
  64.6 3.6 %collective-permute-start.18 = (bf16[576,256]{1,0:T(8,128)(2,1)S(1)}, bf16[576,256]{1,0:T(8,128)(2,1)S(1)}, u32[]{:S(2)}, u32[]{:S(2)}) collective-permute-start(bf16[576,256]{1,0:T(8,128)(2,1)S(1)} %get-tuple-element.33), channel_id=1, source_target_pairs={{0,144},{16,160},{32,176},{48,192},{64,208},{80,224},{96,240},{112... | collective-permute-start | bytes 884744 | tf_op jit(solution)/shard_map/ppermute | solution.py:22
  68.6 3.5 %collective-permute-start.20 = (bf16[576,256]{1,0:T(8,128)(2,1)S(1)}, bf16[576,256]{1,0:T(8,128)(2,1)S(1)}, u32[]{:S(2)}, u32[]{:S(2)}) collective-permute-start(bf16[576,256]{1,0:T(8,128)(2,1)S(1)} %get-tuple-element.35), channel_id=1, source_target_pairs={{0,16},{16,32},{32,48},{48,64},{64,80},{80,96},{96,112},{112,128},... | collective-permute-start | bytes 884744 | tf_op jit(solution)/shard_map/ppermute | solution.py:22
  73.4 3.6 %collective-permute-done.18 = bf16[576,256]{1,0:T(8,128)(2,1)S(1)} collective-permute-done((bf16[576,256]{1,0:T(8,128)(2,1)S(1)}, bf16[576,256]{1,0:T(8,128)(2,1)S(1)}, u32[]{:S(2)}, u32[]{:S(2)}) %collective-permute-start.18) | collective-permute-done | bytes 294944 | tf_op jit(solution)/shard_map/ppermute | solution.py:22
  77.0 4.4 %collective-permute-done.19 = bf16[576,256]{1,0:T(8,128)(2,1)S(1)} collective-permute-done((bf16[576,256]{1,0:T(8,128)(2,1)S(1)}, bf16[576,256]{1,0:T(8,128)(2,1)S(1)}, u32[]{:S(2)}, u32[]{:S(2)}) %collective-permute-start.19) | collective-permute-done | bytes 294944 | tf_op jit(solution)/shard_map/ppermute | solution.py:22
  81.4 4.7 %collective-permute-done.20 = bf16[576,256]{1,0:T(8,128)(2,1)S(1)} collective-permute-done((bf16[576,256]{1,0:T(8,128)(2,1)S(1)}, bf16[576,256]{1,0:T(8,128)(2,1)S(1)}, u32[]{:S(2)}, u32[]{:S(2)}) %collective-permute-start.20) | collective-permute-done | bytes 294944 | tf_op jit(solution)/shard_map/ppermute | solution.py:22
  (36 shorter events, 11.1 us)
Async XLA Ops:
  0.7 1.0 %copy-start = (bf16[256,576]{0,1:T(8,128)(2,1)S(1)}, bf16[256,576]{0,1:T(8,128)(2,1)}, u32[]{:S(2)}) copy-start(bf16[256,576]{0,1:T(8,128)(2,1)} %param.3) | copy-start | bytes 884740
  1.6 10.3 %collective-permute-start.3 = (bf16[592,256]{1,0:T(8,128)(2,1)S(1)}, bf16[592,256]{1,0:T(8,128)(2,1)S(1)}, u32[]{:S(2)}, u32[]{:S(2)}) collective-permute-start(bf16[592,256]{1,0:T(8,128)(2,1)S(1)} %shard_map.37.own_ref.refs_0_), channel_id=1, source_target_pairs={{0,112},{16,128},{32,144},{48,160},{64,176},{80,192},{96,208},{112... | collective-permute-start | bytes 909320 | tf_op jit(solution)/shard_map/ppermute | solution.py:22
  6.0 11.0 %collective-permute-start.2 = (bf16[592,256]{1,0:T(8,128)(2,1)S(1)}, bf16[592,256]{1,0:T(8,128)(2,1)S(1)}, u32[]{:S(2)}, u32[]{:S(2)}) collective-permute-start(bf16[592,256]{1,0:T(8,128)(2,1)S(1)} %shard_map.37.own_ref.refs_0_), channel_id=1, source_target_pairs={{0,208},{16,224},{32,240},{48,0},{64,16},{80,32},{96,48},{112,64},... | collective-permute-start | bytes 909320 | tf_op jit(solution)/shard_map/ppermute | solution.py:22
  7.1 12.8 %collective-permute-start.1 = (bf16[592,256]{1,0:T(8,128)(2,1)S(1)}, bf16[592,256]{1,0:T(8,128)(2,1)S(1)}, u32[]{:S(2)}, u32[]{:S(2)}) collective-permute-start(bf16[592,256]{1,0:T(8,128)(2,1)S(1)} %shard_map.37.own_ref.refs_0_), channel_id=1, source_target_pairs={{0,64},{16,80},{32,96},{48,112},{64,128},{80,144},{96,160},{112,17... | collective-permute-start | bytes 909320 | tf_op jit(solution)/shard_map/ppermute | solution.py:22
  7.8 12.1 %collective-permute-start = (bf16[592,256]{1,0:T(8,128)(2,1)S(1)}, bf16[592,256]{1,0:T(8,128)(2,1)S(1)}, u32[]{:S(2)}, u32[]{:S(2)}) collective-permute-start(bf16[592,256]{1,0:T(8,128)(2,1)S(1)} %shard_map.37.own_ref.refs_0_), channel_id=1, source_target_pairs={{0,240},{16,0},{32,16},{48,32},{64,48},{80,64},{96,80},{112,96},{1... | collective-permute-start | bytes 909320 | tf_op jit(solution)/shard_map/ppermute | solution.py:22
  20.8 3.1 %collective-permute-start.4 = (bf16[1152,256]{1,0:T(8,128)(2,1)S(1)}, bf16[1152,256]{1,0:T(8,128)(2,1)S(1)}, u32[]{:S(2)}, u32[]{:S(2)}) collective-permute-start(bf16[1152,256]{1,0:T(8,128)(2,1)S(1)} %get-tuple-element.24), channel_id=1, source_target_pairs={{0,1},{1,0},{2,3},{3,2},{4,5},{5,4},{6,7},{7,6},{8,9},{9,8},{10,11... | collective-permute-start | bytes 1769480 | tf_op jit(solution)/shard_map/ppermute | solution.py:33
  23.9 21.4 %copy-start.1 = (f32[256]{0:T(256)S(1)}, f32[256]{0:T(256)}, u32[]{:S(2)}) copy-start(f32[256]{0:T(256)} %param.5) | copy-start | bytes 3076
  24.0 10.1 %collective-permute-start.6 = (bf16[288,256]{1,0:T(8,128)(2,1)S(1)}, bf16[288,256]{1,0:T(8,128)(2,1)S(1)}, u32[]{:S(2)}, u32[]{:S(2)}) collective-permute-start(bf16[288,256]{1,0:T(8,128)(2,1)S(1)} %get-tuple-element.28), channel_id=1, source_target_pairs={{0,2},{1,15},{2,4},{3,1},{4,6},{5,3},{6,8},{7,5},{8,10},{9,7},{10,... | collective-permute-start | bytes 442376 | tf_op jit(solution)/shard_map/ppermute | solution.py:29
  29.6 4.4 %collective-permute-start.7 = (bf16[144,256]{1,0:T(8,128)(2,1)S(1)}, bf16[144,256]{1,0:T(8,128)(2,1)S(1)}, u32[]{:S(2)}, u32[]{:S(2)}) collective-permute-start(bf16[144,256]{1,0:T(8,128)(2,1)S(1)} %get-tuple-element.29), channel_id=1, source_target_pairs={{0,4},{1,13},{2,6},{3,15},{4,8},{5,1},{6,10},{7,3},{8,12},{9,5},{1... | collective-permute-start | bytes 221192 | tf_op jit(solution)/shard_map/ppermute | solution.py:29
  30.8 6.5 %collective-permute-start.5 = (bf16[288,256]{1,0:T(8,128)(2,1)S(1)}, bf16[288,256]{1,0:T(8,128)(2,1)S(1)}, u32[]{:S(2)}, u32[]{:S(2)}) collective-permute-start(bf16[288,256]{1,0:T(8,128)(2,1)S(1)} %get-tuple-element.26), channel_id=1, source_target_pairs={{0,2},{1,15},{2,4},{3,1},{4,6},{5,3},{6,8},{7,5},{8,10},{9,7},{10,... | collective-permute-start | bytes 442376 | tf_op jit(solution)/shard_map/ppermute | solution.py:29
  34.1 6.6 %collective-permute-start.8 = (bf16[288,256]{1,0:T(8,128)(2,1)S(1)}, bf16[288,256]{1,0:T(8,128)(2,1)S(1)}, u32[]{:S(2)}, u32[]{:S(2)}) collective-permute-start(bf16[288,256]{1,0:T(8,128)(2,1)S(1)} %shard_map.41), channel_id=1, source_target_pairs={{0,4},{1,13},{2,6},{3,15},{4,8},{5,1},{6,10},{7,3},{8,12},{9,5},{1... | collective-permute-start | bytes 442376 | tf_op jit(solution)/shard_map/ppermute | solution.py:29
  40.7 5.8 %collective-permute-start.9 = (f32[288,256]{1,0:T(8,128)S(1)}, f32[288,256]{1,0:T(8,128)S(1)}, u32[]{:S(2)}, u32[]{:S(2)}) collective-permute-start(f32[288,256]{1,0:T(8,128)S(1)} %shard_map.42.refs_5_), channel_id=1, source_target_pairs={{0,1},{1,0},{2,3},{3,2},{4,5},{5,4},{6,7},{7,6},{8,9},{9,8},{10,11... | collective-permute-start | bytes 884744 | tf_op jit(solution)/shard_map/ppermute | solution.py:33
  46.6 5.3 %collective-permute-start.11 = (bf16[288,256]{1,0:T(8,128)(2,1)S(1)}, bf16[288,256]{1,0:T(8,128)(2,1)S(1)}, u32[]{:S(2)}, u32[]{:S(2)}) collective-permute-start(bf16[288,256]{1,0:T(8,128)(2,1)S(1)} %shard_map.44.refs_5_), channel_id=1, source_target_pairs={{0,4},{1,13},{2,6},{3,15},{4,8},{5,1},{6,10},{7,3},{8,12},{9,5},{1... | collective-permute-start | bytes 442376 | tf_op jit(solution)/shard_map/ppermute | solution.py:29
  46.6 8.7 %collective-permute-start.10 = (bf16[288,256]{1,0:T(8,128)(2,1)S(1)}, bf16[288,256]{1,0:T(8,128)(2,1)S(1)}, u32[]{:S(2)}, u32[]{:S(2)}) collective-permute-start(bf16[288,256]{1,0:T(8,128)(2,1)S(1)} %shard_map.44.refs_5_), channel_id=1, source_target_pairs={{0,2},{1,15},{2,4},{3,1},{4,6},{5,3},{6,8},{7,5},{8,10},{9,7},{10,... | collective-permute-start | bytes 442376 | tf_op jit(solution)/shard_map/ppermute | solution.py:29
  51.9 5.5 %collective-permute-start.12 = (bf16[288,256]{1,0:T(8,128)(2,1)S(1)}, bf16[288,256]{1,0:T(8,128)(2,1)S(1)}, u32[]{:S(2)}, u32[]{:S(2)}) collective-permute-start(bf16[288,256]{1,0:T(8,128)(2,1)S(1)} %collective-permute-done.11.refs_7_), channel_id=1, source_target_pairs={{0,2},{1,15},{2,4},{3,1},{4,6},{5,3},{6,8},{7,5},{8,10},{9,7},{10,... | collective-permute-start | bytes 442376 | tf_op jit(solution)/shard_map/ppermute | solution.py:29
  54.5 7.7 %collective-permute-start.13 = (bf16[144,256]{1,0:T(8,128)(2,1)S(1)}, bf16[144,256]{1,0:T(8,128)(2,1)S(1)}, u32[]{:S(2)}, u32[]{:S(2)}) collective-permute-start(bf16[144,256]{1,0:T(8,128)(2,1)S(1)} %slice.4), channel_id=1, source_target_pairs={{0,4},{1,13},{2,6},{3,15},{4,8},{5,1},{6,10},{7,3},{8,12},{9,5},{1... | collective-permute-start | bytes 221192 | tf_op jit(solution)/shard_map/ppermute | solution.py:29
  54.5 8.9 %collective-permute-start.15 = (bf16[288,256]{1,0:T(8,128)(2,1)S(1)}, bf16[288,256]{1,0:T(8,128)(2,1)S(1)}, u32[]{:S(2)}, u32[]{:S(2)}) collective-permute-start(bf16[288,256]{1,0:T(8,128)(2,1)S(1)} %collective-permute-done.11.refs_7_), channel_id=1, source_target_pairs={{0,1},{1,0},{2,3},{3,2},{4,5},{5,4},{6,7},{7,6},{8,9},{9,8},{10,11... | collective-permute-start | bytes 442376 | tf_op jit(solution)/shard_map/ppermute | solution.py:33
  55.4 8.0 %collective-permute-start.14 = (bf16[288,256]{1,0:T(8,128)(2,1)S(1)}, bf16[288,256]{1,0:T(8,128)(2,1)S(1)}, u32[]{:S(2)}, u32[]{:S(2)}) collective-permute-start(bf16[288,256]{1,0:T(8,128)(2,1)S(1)} %collective-permute-done.10.refs_6_), channel_id=1, source_target_pairs={{0,1},{1,0},{2,3},{3,2},{4,5},{5,4},{6,7},{7,6},{8,9},{9,8},{10,11... | collective-permute-start | bytes 442376 | tf_op jit(solution)/shard_map/ppermute | solution.py:33
  57.3 6.1 %collective-permute-start.16 = (bf16[288,256]{1,0:T(8,128)(2,1)S(1)}, bf16[288,256]{1,0:T(8,128)(2,1)S(1)}, u32[]{:S(2)}, u32[]{:S(2)}) collective-permute-start(bf16[288,256]{1,0:T(8,128)(2,1)S(1)} %collective-permute-done.12.refs_8_), channel_id=1, source_target_pairs={{0,1},{1,0},{2,3},{3,2},{4,5},{5,4},{6,7},{7,6},{8,9},{9,8},{10,11... | collective-permute-start | bytes 442376 | tf_op jit(solution)/shard_map/ppermute | solution.py:33
  62.1 1.3 %collective-permute-start.17 = (bf16[144,256]{1,0:T(8,128)(2,1)S(1)}, bf16[144,256]{1,0:T(8,128)(2,1)S(1)}, u32[]{:S(2)}, u32[]{:S(2)}) collective-permute-start(bf16[144,256]{1,0:T(8,128)(2,1)S(1)} %collective-permute-done.13.refs_9_), channel_id=1, source_target_pairs={{0,1},{1,0},{2,3},{3,2},{4,5},{5,4},{6,7},{7,6},{8,9},{9,8},{10,11... | collective-permute-start | bytes 221192 | tf_op jit(solution)/shard_map/ppermute | solution.py:33
  64.6 12.4 %collective-permute-start.18 = (bf16[576,256]{1,0:T(8,128)(2,1)S(1)}, bf16[576,256]{1,0:T(8,128)(2,1)S(1)}, u32[]{:S(2)}, u32[]{:S(2)}) collective-permute-start(bf16[576,256]{1,0:T(8,128)(2,1)S(1)} %get-tuple-element.33), channel_id=1, source_target_pairs={{0,144},{16,160},{32,176},{48,192},{64,208},{80,224},{96,240},{112... | collective-permute-start | bytes 884744 | tf_op jit(solution)/shard_map/ppermute | solution.py:22
  68.2 13.2 %collective-permute-start.19 = (bf16[576,256]{1,0:T(8,128)(2,1)S(1)}, bf16[576,256]{1,0:T(8,128)(2,1)S(1)}, u32[]{:S(2)}, u32[]{:S(2)}) collective-permute-start(bf16[576,256]{1,0:T(8,128)(2,1)S(1)} %get-tuple-element.34), channel_id=1, source_target_pairs={{0,48},{16,64},{32,80},{48,96},{64,112},{80,128},{96,144},{112,160... | collective-permute-start | bytes 884744 | tf_op jit(solution)/shard_map/ppermute | solution.py:22
  68.6 17.5 %collective-permute-start.20 = (bf16[576,256]{1,0:T(8,128)(2,1)S(1)}, bf16[576,256]{1,0:T(8,128)(2,1)S(1)}, u32[]{:S(2)}, u32[]{:S(2)}) collective-permute-start(bf16[576,256]{1,0:T(8,128)(2,1)S(1)} %get-tuple-element.35), channel_id=1, source_target_pairs={{0,16},{16,32},{32,48},{48,64},{64,80},{80,96},{96,112},{112,128},... | collective-permute-start | bytes 884744 | tf_op jit(solution)/shard_map/ppermute | solution.py:22
  72.2 13.9 %collective-permute-start.21 = (bf16[576,256]{1,0:T(8,128)(2,1)S(1)}, bf16[576,256]{1,0:T(8,128)(2,1)S(1)}, u32[]{:S(2)}, u32[]{:S(2)}) collective-permute-start(bf16[576,256]{1,0:T(8,128)(2,1)S(1)} %get-tuple-element.36), channel_id=1, source_target_pairs={{0,192},{16,208},{32,224},{48,240},{64,0},{80,16},{96,32},{112,48}... | collective-permute-start | bytes 884744 | tf_op jit(solution)/shard_map/ppermute | solution.py:22

commit v3 on v1

--- a/solution.py
+++ b/solution.py
@@ -125,7 +125,7 @@
 
 
 def gamma_kernel(depth, *refs):
-    blocks, own, mine, other, outs, whole = refs[:5], refs[5], refs[6:10], refs[10:14], refs[14:18], refs[18]
+    blocks, own, mine, other, outs, whole = refs[:5], refs[5], refs[6:10], refs[10:13], refs[13:17], refs[17]
     z, core = place()
     way = 1 - 2 * core
     for r in range(len(PAIRS)):
@@ -209,13 +209,13 @@
     two = along_z(amplitude, 2)
     one = along_z(amplitude, 1)
     three = along_z(two, 1)
-    four = along_z(two[:SIZE], 2)
+    four = along_z(two, 2)
     mine = [one, two, three, four]
-    other = [sibling(piece) for piece in mine]
+    other = [sibling(piece) for piece in mine[:3]]
 
     parts = call(
         functools.partial(gamma_kernel, depth),
-        [VMEM] * 14,
+        [VMEM] * 13,
         [shape((depth, width), bf16)] * 4 + [shape((len(PAIRS), width, width), bf16)],
     )(*blocks, amplitude, *mine, *other)
     *parts, whole = parts

time: 86.5 us -> 86.8 us (level)
  starting transfers between devices: 44.7 us -> 46.9 us
  waiting for transfers between devices: 35.4 us -> 33.5 us
    ppermute x8, waiting for transfers between devices: 11.3 us -> 9.79 us  [along_z(): return lax.ppermute(array, 'aux', [(i, target(i)) for i in range(16)])]
    ppermute x6 -> x5, starting transfers between devices: 11.8 us -> 12.9 us  [sibling(): return lax.ppermute(array, 'aux', [(i, i ^ 1) for i in range(16)])]
    ppermute x8, starting transfers between devices: 15.2 us -> 16.3 us  [along_z(): return lax.ppermute(array, 'aux', [(i, target(i)) for i in range(16)])]
    ppermute x6 -> x5, waiting for transfers between devices: 4 us -> 3.73 us  [sibling(): return lax.ppermute(array, 'aux', [(i, i ^ 1) for i in range(16)])]
  transfers between devices with their start and end apart: 22 -> 21, of which waited for: 14 -> 14; matrix products, arithmetic and copies ran while one was open for 0% -> 0% of each run, Pallas kernels for 2% -> 2%
where the time goes in v3:
time: 86.8 us; the launch traced here: 86.7 us
  starting transfers between devices  46.9 us (54%)
  waiting for transfers between devices  33.5 us (39%)
  Pallas kernels  3.57 us (4%)
  other arithmetic  0.97 us (1%)
  local copies, waits for them, and re-layouts  0.96 us (1%)
    ppermute x8, waiting for transfers between devices, send_home(): return lax.ppermute(array, 'occ', [(i, (i + by) % 16) for i in range(16)])  20 us
    ppermute x8, starting transfers between devices, send_home(): return lax.ppermute(array, 'occ', [(i, (i + by) % 16) for i in range(16)])  17.7 us
    ppermute x8, starting transfers between devices, along_z(): return lax.ppermute(array, 'aux', [(i, target(i)) for i in range(16)])  16.3 us
    ppermute x5, starting transfers between devices, sibling(): return lax.ppermute(array, 'aux', [(i, i ^ 1) for i in range(16)])  12.9 us
    ppermute x8, waiting for transfers between devices, along_z(): return lax.ppermute(array, 'aux', [(i, target(i)) for i in range(16)])  9.79 us
    ppermute x5, waiting for transfers between devices, sibling(): return lax.ppermute(array, 'aux', [(i, i ^ 1) for i in range(16)])  3.73 us
  transfers between devices with their start and end apart: 21, of which 14 were waited for; matrix products, arithmetic and copies ran while one was open for 0% of the time, Pallas kernels for 2%

profile of v3, /device:TPU:1, one launch (start us, length us, event | category | flops | bytes accessed | tf_op | source)
XLA Modules:
  0.0 86.7 jit_solution(3416144723672664521)
XLA Ops:
  1.6 4.4 %collective-permute-start.3 = (bf16[592,256]{1,0:T(8,128)(2,1)S(1)}, bf16[592,256]{1,0:T(8,128)(2,1)S(1)}, u32[]{:S(2)}, u32[]{:S(2)}) collective-permute-start(bf16[592,256]{1,0:T(8,128)(2,1)S(1)} %shard_map.37.own_ref.refs_0_), channel_id=1, source_target_pairs={{0,112},{16,128},{32,144},{48,160},{64,176},{80,192},{96,208},{112... | collective-permute-start | bytes 909320 | tf_op jit(solution)/shard_map/ppermute | solution.py:22
  7.8 3.3 %collective-permute-start = (bf16[592,256]{1,0:T(8,128)(2,1)S(1)}, bf16[592,256]{1,0:T(8,128)(2,1)S(1)}, u32[]{:S(2)}, u32[]{:S(2)}) collective-permute-start(bf16[592,256]{1,0:T(8,128)(2,1)S(1)} %shard_map.37.own_ref.refs_0_), channel_id=1, source_target_pairs={{0,240},{16,0},{32,16},{48,32},{64,48},{80,64},{96,80},{112,96},{1... | collective-permute-start | bytes 909320 | tf_op jit(solution)/shard_map/ppermute | solution.py:22
  11.9 5.1 %collective-permute-done.2.third_ref.refs_3_ = bf16[592,256]{1,0:T(8,128)(2,1)S(1)} collective-permute-done((bf16[592,256]{1,0:T(8,128)(2,1)S(1)}, bf16[592,256]{1,0:T(8,128)(2,1)S(1)}, u32[]{:S(2)}, u32[]{:S(2)}) %collective-permute-start.2) | collective-permute-done | bytes 303136 | tf_op jit(solution)/shard_map/ppermute | solution.py:22
  17.7 2.3 %collective-permute-done.1.refs_2_ = bf16[592,256]{1,0:T(8,128)(2,1)S(1)} collective-permute-done((bf16[592,256]{1,0:T(8,128)(2,1)S(1)}, bf16[592,256]{1,0:T(8,128)(2,1)S(1)}, u32[]{:S(2)}, u32[]{:S(2)}) %collective-permute-start.1) | collective-permute-done | bytes 303136 | tf_op jit(solution)/shard_map/ppermute | solution.py:22
  20.8 1.4 %collective-permute-start.4 = (bf16[1152,256]{1,0:T(8,128)(2,1)S(1)}, bf16[1152,256]{1,0:T(8,128)(2,1)S(1)}, u32[]{:S(2)}, u32[]{:S(2)}) collective-permute-start(bf16[1152,256]{1,0:T(8,128)(2,1)S(1)} %get-tuple-element.24), channel_id=1, source_target_pairs={{0,1},{1,0},{2,3},{3,2},{4,5},{5,4},{6,7},{7,6},{8,9},{9,8},{10,11... | collective-permute-start | bytes 1769480 | tf_op jit(solution)/shard_map/ppermute | solution.py:33
  22.3 1.6 %collective-permute-done.4.got_ref = bf16[1152,256]{1,0:T(8,128)(2,1)S(1)} collective-permute-done((bf16[1152,256]{1,0:T(8,128)(2,1)S(1)}, bf16[1152,256]{1,0:T(8,128)(2,1)S(1)}, u32[]{:S(2)}, u32[]{:S(2)}) %collective-permute-start.4) | collective-permute-done | bytes 589856 | tf_op jit(solution)/shard_map/ppermute | solution.py:33
  24.0 5.7 %collective-permute-start.6 = (bf16[288,256]{1,0:T(8,128)(2,1)S(1)}, bf16[288,256]{1,0:T(8,128)(2,1)S(1)}, u32[]{:S(2)}, u32[]{:S(2)}) collective-permute-start(bf16[288,256]{1,0:T(8,128)(2,1)S(1)} %get-tuple-element.28), channel_id=1, source_target_pairs={{0,2},{1,15},{2,4},{3,1},{4,6},{5,3},{6,8},{7,5},{8,10},{9,7},{10,... | collective-permute-start | bytes 442376 | tf_op jit(solution)/shard_map/ppermute | solution.py:29
  29.6 1.2 %collective-permute-start.7 = (bf16[144,256]{1,0:T(8,128)(2,1)S(1)}, bf16[144,256]{1,0:T(8,128)(2,1)S(1)}, u32[]{:S(2)}, u32[]{:S(2)}) collective-permute-start(bf16[144,256]{1,0:T(8,128)(2,1)S(1)} %get-tuple-element.29), channel_id=1, source_target_pairs={{0,4},{1,13},{2,6},{3,15},{4,8},{5,1},{6,10},{7,3},{8,12},{9,5},{1... | collective-permute-start | bytes 221192 | tf_op jit(solution)/shard_map/ppermute | solution.py:29
  31.5 2.5 %collective-permute-done.7.four_ref = bf16[144,256]{1,0:T(8,128)(2,1)S(1)} collective-permute-done((bf16[144,256]{1,0:T(8,128)(2,1)S(1)}, bf16[144,256]{1,0:T(8,128)(2,1)S(1)}, u32[]{:S(2)}, u32[]{:S(2)}) %collective-permute-start.7) | collective-permute-done | bytes 73760 | tf_op jit(solution)/shard_map/ppermute | solution.py:29
  34.1 3.2 %collective-permute-start.8 = (bf16[288,256]{1,0:T(8,128)(2,1)S(1)}, bf16[288,256]{1,0:T(8,128)(2,1)S(1)}, u32[]{:S(2)}, u32[]{:S(2)}) collective-permute-start(bf16[288,256]{1,0:T(8,128)(2,1)S(1)} %shard_map.41), channel_id=1, source_target_pairs={{0,4},{1,13},{2,6},{3,15},{4,8},{5,1},{6,10},{7,3},{8,12},{9,5},{1... | collective-permute-start | bytes 442376 | tf_op jit(solution)/shard_map/ppermute | solution.py:29
  37.3 3.4 %collective-permute-done.8.two_ref = bf16[288,256]{1,0:T(8,128)(2,1)S(1)} collective-permute-done((bf16[288,256]{1,0:T(8,128)(2,1)S(1)}, bf16[288,256]{1,0:T(8,128)(2,1)S(1)}, u32[]{:S(2)}, u32[]{:S(2)}) %collective-permute-start.8) | collective-permute-done | bytes 147488 | tf_op jit(solution)/shard_map/ppermute | solution.py:29
  40.7 4.5 %collective-permute-start.9 = (f32[288,256]{1,0:T(8,128)S(1)}, f32[288,256]{1,0:T(8,128)S(1)}, u32[]{:S(2)}, u32[]{:S(2)}) collective-permute-start(f32[288,256]{1,0:T(8,128)S(1)} %shard_map.42.refs_5_), channel_id=1, source_target_pairs={{0,1},{1,0},{2,3},{3,2},{4,5},{5,4},{6,7},{7,6},{8,9},{9,8},{10,11... | collective-permute-start | bytes 884744 | tf_op jit(solution)/shard_map/ppermute | solution.py:33
  46.6 1.7 %collective-permute-start.10 = (bf16[288,256]{1,0:T(8,128)(2,1)S(1)}, bf16[288,256]{1,0:T(8,128)(2,1)S(1)}, u32[]{:S(2)}, u32[]{:S(2)}) collective-permute-start(bf16[288,256]{1,0:T(8,128)(2,1)S(1)} %shard_map.44.refs_5_), channel_id=1, source_target_pairs={{0,2},{1,15},{2,4},{3,1},{4,6},{5,3},{6,8},{7,5},{8,10},{9,7},{10,... | collective-permute-start | bytes 442376 | tf_op jit(solution)/shard_map/ppermute | solution.py:29
  48.3 3.5 %collective-permute-done.11.refs_7_ = bf16[288,256]{1,0:T(8,128)(2,1)S(1)} collective-permute-done((bf16[288,256]{1,0:T(8,128)(2,1)S(1)}, bf16[288,256]{1,0:T(8,128)(2,1)S(1)}, u32[]{:S(2)}, u32[]{:S(2)}) %collective-permute-start.11) | collective-permute-done | bytes 147488 | tf_op jit(solution)/shard_map/ppermute | solution.py:29
  51.9 2.6 %collective-permute-start.12 = (bf16[288,256]{1,0:T(8,128)(2,1)S(1)}, bf16[288,256]{1,0:T(8,128)(2,1)S(1)}, u32[]{:S(2)}, u32[]{:S(2)}) collective-permute-start(bf16[288,256]{1,0:T(8,128)(2,1)S(1)} %collective-permute-done.11.refs_7_), channel_id=1, source_target_pairs={{0,2},{1,15},{2,4},{3,1},{4,6},{5,3},{6,8},{7,5},{8,10},{9,7},{10,... | collective-permute-start | bytes 442376 | tf_op jit(solution)/shard_map/ppermute | solution.py:29
  55.0 1.2 %collective-permute-start.13 = (bf16[288,256]{1,0:T(8,128)(2,1)S(1)}, bf16[288,256]{1,0:T(8,128)(2,1)S(1)}, u32[]{:S(2)}, u32[]{:S(2)}) collective-permute-start(bf16[288,256]{1,0:T(8,128)(2,1)S(1)} %collective-permute-done.11.refs_7_), channel_id=1, source_target_pairs={{0,4},{1,13},{2,6},{3,15},{4,8},{5,1},{6,10},{7,3},{8,12},{9,5},{1... | collective-permute-start | bytes 442376 | tf_op jit(solution)/shard_map/ppermute | solution.py:29
  56.6 6.4 %collective-permute-start.16 = (bf16[288,256]{1,0:T(8,128)(2,1)S(1)}, bf16[288,256]{1,0:T(8,128)(2,1)S(1)}, u32[]{:S(2)}, u32[]{:S(2)}) collective-permute-start(bf16[288,256]{1,0:T(8,128)(2,1)S(1)} %collective-permute-done.12.refs_8_), channel_id=1, source_target_pairs={{0,1},{1,0},{2,3},{3,2},{4,5},{5,4},{6,7},{7,6},{8,9},{9,8},{10,11... | collective-permute-start | bytes 442376 | tf_op jit(solution)/shard_map/ppermute | solution.py:33
  65.1 3.6 %collective-permute-start.17 = (bf16[576,256]{1,0:T(8,128)(2,1)S(1)}, bf16[576,256]{1,0:T(8,128)(2,1)S(1)}, u32[]{:S(2)}, u32[]{:S(2)}) collective-permute-start(bf16[576,256]{1,0:T(8,128)(2,1)S(1)} %get-tuple-element.33), channel_id=1, source_target_pairs={{0,144},{16,160},{32,176},{48,192},{64,208},{80,224},{96,240},{112... | collective-permute-start | bytes 884744 | tf_op jit(solution)/shard_map/ppermute | solution.py:22
  69.1 3.0 %collective-permute-start.19 = (bf16[576,256]{1,0:T(8,128)(2,1)S(1)}, bf16[576,256]{1,0:T(8,128)(2,1)S(1)}, u32[]{:S(2)}, u32[]{:S(2)}) collective-permute-start(bf16[576,256]{1,0:T(8,128)(2,1)S(1)} %get-tuple-element.35), channel_id=1, source_target_pairs={{0,192},{16,208},{32,224},{48,240},{64,0},{80,16},{96,32},{112,48}... | collective-permute-start | bytes 884744 | tf_op jit(solution)/shard_map/ppermute | solution.py:22
  72.1 1.2 %collective-permute-start.20 = (bf16[576,256]{1,0:T(8,128)(2,1)S(1)}, bf16[576,256]{1,0:T(8,128)(2,1)S(1)}, u32[]{:S(2)}, u32[]{:S(2)}) collective-permute-start(bf16[576,256]{1,0:T(8,128)(2,1)S(1)} %get-tuple-element.36), channel_id=1, source_target_pairs={{0,16},{16,32},{32,48},{48,64},{64,80},{80,96},{96,112},{112,128},... | collective-permute-start | bytes 884744 | tf_op jit(solution)/shard_map/ppermute | solution.py:22
  73.9 3.2 %collective-permute-done.17 = bf16[576,256]{1,0:T(8,128)(2,1)S(1)} collective-permute-done((bf16[576,256]{1,0:T(8,128)(2,1)S(1)}, bf16[576,256]{1,0:T(8,128)(2,1)S(1)}, u32[]{:S(2)}, u32[]{:S(2)}) %collective-permute-start.17) | collective-permute-done | bytes 294944 | tf_op jit(solution)/shard_map/ppermute | solution.py:22
  77.1 4.1 %collective-permute-done.18 = bf16[576,256]{1,0:T(8,128)(2,1)S(1)} collective-permute-done((bf16[576,256]{1,0:T(8,128)(2,1)S(1)}, bf16[576,256]{1,0:T(8,128)(2,1)S(1)}, u32[]{:S(2)}, u32[]{:S(2)}) %collective-permute-start.18) | collective-permute-done | bytes 294944 | tf_op jit(solution)/shard_map/ppermute | solution.py:22
  81.3 1.9 %collective-permute-done.19 = bf16[576,256]{1,0:T(8,128)(2,1)S(1)} collective-permute-done((bf16[576,256]{1,0:T(8,128)(2,1)S(1)}, bf16[576,256]{1,0:T(8,128)(2,1)S(1)}, u32[]{:S(2)}, u32[]{:S(2)}) %collective-permute-start.19) | collective-permute-done | bytes 294944 | tf_op jit(solution)/shard_map/ppermute | solution.py:22
  83.1 2.6 %collective-permute-done.20 = bf16[576,256]{1,0:T(8,128)(2,1)S(1)} collective-permute-done((bf16[576,256]{1,0:T(8,128)(2,1)S(1)}, bf16[576,256]{1,0:T(8,128)(2,1)S(1)}, u32[]{:S(2)}, u32[]{:S(2)}) %collective-permute-start.20) | collective-permute-done | bytes 294944 | tf_op jit(solution)/shard_map/ppermute | solution.py:22
  (33 shorter events, 12.4 us)
Async XLA Ops:
  0.7 1.0 %copy-start = (bf16[256,576]{0,1:T(8,128)(2,1)S(1)}, bf16[256,576]{0,1:T(8,128)(2,1)}, u32[]{:S(2)}) copy-start(bf16[256,576]{0,1:T(8,128)(2,1)} %param.3) | copy-start | bytes 884740
  1.6 10.3 %collective-permute-start.3 = (bf16[592,256]{1,0:T(8,128)(2,1)S(1)}, bf16[592,256]{1,0:T(8,128)(2,1)S(1)}, u32[]{:S(2)}, u32[]{:S(2)}) collective-permute-start(bf16[592,256]{1,0:T(8,128)(2,1)S(1)} %shard_map.37.own_ref.refs_0_), channel_id=1, source_target_pairs={{0,112},{16,128},{32,144},{48,160},{64,176},{80,192},{96,208},{112... | collective-permute-start | bytes 909320 | tf_op jit(solution)/shard_map/ppermute | solution.py:22
  6.0 11.0 %collective-permute-start.2 = (bf16[592,256]{1,0:T(8,128)(2,1)S(1)}, bf16[592,256]{1,0:T(8,128)(2,1)S(1)}, u32[]{:S(2)}, u32[]{:S(2)}) collective-permute-start(bf16[592,256]{1,0:T(8,128)(2,1)S(1)} %shard_map.37.own_ref.refs_0_), channel_id=1, source_target_pairs={{0,208},{16,224},{32,240},{48,0},{64,16},{80,32},{96,48},{112,64},... | collective-permute-start | bytes 909320 | tf_op jit(solution)/shard_map/ppermute | solution.py:22
  7.1 12.8 %collective-permute-start.1 = (bf16[592,256]{1,0:T(8,128)(2,1)S(1)}, bf16[592,256]{1,0:T(8,128)(2,1)S(1)}, u32[]{:S(2)}, u32[]{:S(2)}) collective-permute-start(bf16[592,256]{1,0:T(8,128)(2,1)S(1)} %shard_map.37.own_ref.refs_0_), channel_id=1, source_target_pairs={{0,64},{16,80},{32,96},{48,112},{64,128},{80,144},{96,160},{112,17... | collective-permute-start | bytes 909320 | tf_op jit(solution)/shard_map/ppermute | solution.py:22
  7.8 12.1 %collective-permute-start = (bf16[592,256]{1,0:T(8,128)(2,1)S(1)}, bf16[592,256]{1,0:T(8,128)(2,1)S(1)}, u32[]{:S(2)}, u32[]{:S(2)}) collective-permute-start(bf16[592,256]{1,0:T(8,128)(2,1)S(1)} %shard_map.37.own_ref.refs_0_), channel_id=1, source_target_pairs={{0,240},{16,0},{32,16},{48,32},{64,48},{80,64},{96,80},{112,96},{1... | collective-permute-start | bytes 909320 | tf_op jit(solution)/shard_map/ppermute | solution.py:22
  20.8 3.1 %collective-permute-start.4 = (bf16[1152,256]{1,0:T(8,128)(2,1)S(1)}, bf16[1152,256]{1,0:T(8,128)(2,1)S(1)}, u32[]{:S(2)}, u32[]{:S(2)}) collective-permute-start(bf16[1152,256]{1,0:T(8,128)(2,1)S(1)} %get-tuple-element.24), channel_id=1, source_target_pairs={{0,1},{1,0},{2,3},{3,2},{4,5},{5,4},{6,7},{7,6},{8,9},{9,8},{10,11... | collective-permute-start | bytes 1769480 | tf_op jit(solution)/shard_map/ppermute | solution.py:33
  23.9 21.4 %copy-start.1 = (f32[256]{0:T(256)S(1)}, f32[256]{0:T(256)}, u32[]{:S(2)}) copy-start(f32[256]{0:T(256)} %param.5) | copy-start | bytes 3076
  24.0 10.1 %collective-permute-start.6 = (bf16[288,256]{1,0:T(8,128)(2,1)S(1)}, bf16[288,256]{1,0:T(8,128)(2,1)S(1)}, u32[]{:S(2)}, u32[]{:S(2)}) collective-permute-start(bf16[288,256]{1,0:T(8,128)(2,1)S(1)} %get-tuple-element.28), channel_id=1, source_target_pairs={{0,2},{1,15},{2,4},{3,1},{4,6},{5,3},{6,8},{7,5},{8,10},{9,7},{10,... | collective-permute-start | bytes 442376 | tf_op jit(solution)/shard_map/ppermute | solution.py:29
  29.6 4.4 %collective-permute-start.7 = (bf16[144,256]{1,0:T(8,128)(2,1)S(1)}, bf16[144,256]{1,0:T(8,128)(2,1)S(1)}, u32[]{:S(2)}, u32[]{:S(2)}) collective-permute-start(bf16[144,256]{1,0:T(8,128)(2,1)S(1)} %get-tuple-element.29), channel_id=1, source_target_pairs={{0,4},{1,13},{2,6},{3,15},{4,8},{5,1},{6,10},{7,3},{8,12},{9,5},{1... | collective-permute-start | bytes 221192 | tf_op jit(solution)/shard_map/ppermute | solution.py:29
  30.8 6.5 %collective-permute-start.5 = (bf16[288,256]{1,0:T(8,128)(2,1)S(1)}, bf16[288,256]{1,0:T(8,128)(2,1)S(1)}, u32[]{:S(2)}, u32[]{:S(2)}) collective-permute-start(bf16[288,256]{1,0:T(8,128)(2,1)S(1)} %get-tuple-element.26), channel_id=1, source_target_pairs={{0,2},{1,15},{2,4},{3,1},{4,6},{5,3},{6,8},{7,5},{8,10},{9,7},{10,... | collective-permute-start | bytes 442376 | tf_op jit(solution)/shard_map/ppermute | solution.py:29
  34.1 6.6 %collective-permute-start.8 = (bf16[288,256]{1,0:T(8,128)(2,1)S(1)}, bf16[288,256]{1,0:T(8,128)(2,1)S(1)}, u32[]{:S(2)}, u32[]{:S(2)}) collective-permute-start(bf16[288,256]{1,0:T(8,128)(2,1)S(1)} %shard_map.41), channel_id=1, source_target_pairs={{0,4},{1,13},{2,6},{3,15},{4,8},{5,1},{6,10},{7,3},{8,12},{9,5},{1... | collective-permute-start | bytes 442376 | tf_op jit(solution)/shard_map/ppermute | solution.py:29
  40.7 5.8 %collective-permute-start.9 = (f32[288,256]{1,0:T(8,128)S(1)}, f32[288,256]{1,0:T(8,128)S(1)}, u32[]{:S(2)}, u32[]{:S(2)}) collective-permute-start(f32[288,256]{1,0:T(8,128)S(1)} %shard_map.42.refs_5_), channel_id=1, source_target_pairs={{0,1},{1,0},{2,3},{3,2},{4,5},{5,4},{6,7},{7,6},{8,9},{9,8},{10,11... | collective-permute-start | bytes 884744 | tf_op jit(solution)/shard_map/ppermute | solution.py:33
  46.6 5.3 %collective-permute-start.11 = (bf16[288,256]{1,0:T(8,128)(2,1)S(1)}, bf16[288,256]{1,0:T(8,128)(2,1)S(1)}, u32[]{:S(2)}, u32[]{:S(2)}) collective-permute-start(bf16[288,256]{1,0:T(8,128)(2,1)S(1)} %shard_map.44.refs_5_), channel_id=1, source_target_pairs={{0,4},{1,13},{2,6},{3,15},{4,8},{5,1},{6,10},{7,3},{8,12},{9,5},{1... | collective-permute-start | bytes 442376 | tf_op jit(solution)/shard_map/ppermute | solution.py:29
  46.6 9.5 %collective-permute-start.10 = (bf16[288,256]{1,0:T(8,128)(2,1)S(1)}, bf16[288,256]{1,0:T(8,128)(2,1)S(1)}, u32[]{:S(2)}, u32[]{:S(2)}) collective-permute-start(bf16[288,256]{1,0:T(8,128)(2,1)S(1)} %shard_map.44.refs_5_), channel_id=1, source_target_pairs={{0,2},{1,15},{2,4},{3,1},{4,6},{5,3},{6,8},{7,5},{8,10},{9,7},{10,... | collective-permute-start | bytes 442376 | tf_op jit(solution)/shard_map/ppermute | solution.py:29
  51.9 4.7 %collective-permute-start.12 = (bf16[288,256]{1,0:T(8,128)(2,1)S(1)}, bf16[288,256]{1,0:T(8,128)(2,1)S(1)}, u32[]{:S(2)}, u32[]{:S(2)}) collective-permute-start(bf16[288,256]{1,0:T(8,128)(2,1)S(1)} %collective-permute-done.11.refs_7_), channel_id=1, source_target_pairs={{0,2},{1,15},{2,4},{3,1},{4,6},{5,3},{6,8},{7,5},{8,10},{9,7},{10,... | collective-permute-start | bytes 442376 | tf_op jit(solution)/shard_map/ppermute | solution.py:29
  54.5 8.5 %collective-permute-start.15 = (bf16[288,256]{1,0:T(8,128)(2,1)S(1)}, bf16[288,256]{1,0:T(8,128)(2,1)S(1)}, u32[]{:S(2)}, u32[]{:S(2)}) collective-permute-start(bf16[288,256]{1,0:T(8,128)(2,1)S(1)} %collective-permute-done.11.refs_7_), channel_id=1, source_target_pairs={{0,1},{1,0},{2,3},{3,2},{4,5},{5,4},{6,7},{7,6},{8,9},{9,8},{10,11... | collective-permute-start | bytes 442376 | tf_op jit(solution)/shard_map/ppermute | solution.py:33
  55.0 7.9 %collective-permute-start.13 = (bf16[288,256]{1,0:T(8,128)(2,1)S(1)}, bf16[288,256]{1,0:T(8,128)(2,1)S(1)}, u32[]{:S(2)}, u32[]{:S(2)}) collective-permute-start(bf16[288,256]{1,0:T(8,128)(2,1)S(1)} %collective-permute-done.11.refs_7_), channel_id=1, source_target_pairs={{0,4},{1,13},{2,6},{3,15},{4,8},{5,1},{6,10},{7,3},{8,12},{9,5},{1... | collective-permute-start | bytes 442376 | tf_op jit(solution)/shard_map/ppermute | solution.py:29
  56.2 6.8 %collective-permute-start.14 = (bf16[288,256]{1,0:T(8,128)(2,1)S(1)}, bf16[288,256]{1,0:T(8,128)(2,1)S(1)}, u32[]{:S(2)}, u32[]{:S(2)}) collective-permute-start(bf16[288,256]{1,0:T(8,128)(2,1)S(1)} %collective-permute-done.10.refs_6_), channel_id=1, source_target_pairs={{0,1},{1,0},{2,3},{3,2},{4,5},{5,4},{6,7},{7,6},{8,9},{9,8},{10,11... | collective-permute-start | bytes 442376 | tf_op jit(solution)/shard_map/ppermute | solution.py:33
  56.6 7.4 %collective-permute-start.16 = (bf16[288,256]{1,0:T(8,128)(2,1)S(1)}, bf16[288,256]{1,0:T(8,128)(2,1)S(1)}, u32[]{:S(2)}, u32[]{:S(2)}) collective-permute-start(bf16[288,256]{1,0:T(8,128)(2,1)S(1)} %collective-permute-done.12.refs_8_), channel_id=1, source_target_pairs={{0,1},{1,0},{2,3},{3,2},{4,5},{5,4},{6,7},{7,6},{8,9},{9,8},{10,11... | collective-permute-start | bytes 442376 | tf_op jit(solution)/shard_map/ppermute | solution.py:33
  65.1 12.1 %collective-permute-start.17 = (bf16[576,256]{1,0:T(8,128)(2,1)S(1)}, bf16[576,256]{1,0:T(8,128)(2,1)S(1)}, u32[]{:S(2)}, u32[]{:S(2)}) collective-permute-start(bf16[576,256]{1,0:T(8,128)(2,1)S(1)} %get-tuple-element.33), channel_id=1, source_target_pairs={{0,144},{16,160},{32,176},{48,192},{64,208},{80,224},{96,240},{112... | collective-permute-start | bytes 884744 | tf_op jit(solution)/shard_map/ppermute | solution.py:22
  68.7 12.6 %collective-permute-start.18 = (bf16[576,256]{1,0:T(8,128)(2,1)S(1)}, bf16[576,256]{1,0:T(8,128)(2,1)S(1)}, u32[]{:S(2)}, u32[]{:S(2)}) collective-permute-start(bf16[576,256]{1,0:T(8,128)(2,1)S(1)} %get-tuple-element.34), channel_id=1, source_target_pairs={{0,48},{16,64},{32,80},{48,96},{64,112},{80,128},{96,144},{112,160... | collective-permute-start | bytes 884744 | tf_op jit(solution)/shard_map/ppermute | solution.py:22
  69.1 14.0 %collective-permute-start.19 = (bf16[576,256]{1,0:T(8,128)(2,1)S(1)}, bf16[576,256]{1,0:T(8,128)(2,1)S(1)}, u32[]{:S(2)}, u32[]{:S(2)}) collective-permute-start(bf16[576,256]{1,0:T(8,128)(2,1)S(1)} %get-tuple-element.35), channel_id=1, source_target_pairs={{0,192},{16,208},{32,224},{48,240},{64,0},{80,16},{96,32},{112,48}... | collective-permute-start | bytes 884744 | tf_op jit(solution)/shard_map/ppermute | solution.py:22
  72.1 13.6 %collective-permute-start.20 = (bf16[576,256]{1,0:T(8,128)(2,1)S(1)}, bf16[576,256]{1,0:T(8,128)(2,1)S(1)}, u32[]{:S(2)}, u32[]{:S(2)}) collective-permute-start(bf16[576,256]{1,0:T(8,128)(2,1)S(1)} %get-tuple-element.36), channel_id=1, source_target_pairs={{0,16},{16,32},{32,48},{48,64},{64,80},{80,96},{96,112},{112,128},... | collective-permute-start | bytes 884744 | tf_op jit(solution)/shard_map/ppermute | solution.py:22
